TPU v7x, 32 devices: a whole 2x2x4 slice. The times are simulated.
32 devices in a mesh: parts: 2 (over y), inner: 4 (over z), outer: 2 (over x), rep: 2 (over core).
Axes of the slice: x: 2, y: 2, z: 4, core: 2. Of those that a mesh axis runs over, the one named last changes fastest.
Arguments:
- tokens: bfloat16 [512, 1024], P(('parts', 'inner', 'outer'), 'rep'), parts along dimension 0, may hold values from -6 to 6
- teacher: bfloat16 [512, 1024], P(('parts', 'inner', 'outer'), 'rep'), parts along dimension 0, may hold values from -1.5 to 1.5
- expert_ids: int32 [512, 8], P(('parts', 'inner', 'outer')), parts along dimension 0, may hold values from 0 to 7, as said below
- gate_codes: int32 [512, 8], P(('parts', 'inner', 'outer')), parts along dimension 0, may hold values from 49152 to 65535
- gate_up_latent: float32 [8, 2, 384, 1024], P(('inner', 'outer'), None, 'rep'), may hold values from -6 to 6
- down_latent: float32 [8, 384, 1024], P(('inner', 'outer'), 'rep'), may hold values from -6 to 6
Outputs:
- student_out: bfloat16 [512, 1024], P(('parts', 'inner', 'outer'), 'rep'), parts along dimension 0
- new_gate_up: float32 [16, 2, 384, 1024], P(('parts', 'inner', 'outer'), None, 'rep'), parts along dimension 0
- new_down: float32 [16, 384, 1024], P(('parts', 'inner', 'outer'), 'rep'), parts along dimension 0
There are 2 independent parts, one for each index of `parts`. A program takes and returns all parts, laid end to end along the dimension named above; an argument that names none is the same for every part. Nothing has to cross between parts.
Inputs may be any that keep to these rules, and one draw needn't show every extreme that they name: `expert_ids`: each token names 8 different experts. Each aligned block of 32 tokens (the tokens of one device) names any expert at most 32 times, and one expert, the same in every block of a part, exactly 32 times in every block.
All inputs are finite; a program needn't handle non-finite values. Where the computation divides by a largest or mean magnitude, that divisor is 1e-20 or more.
Results may differ from a plain program's by a relative error of at most 0.012.
Values may be sent and summed in bfloat16 or wider, within the bound.
A program may use at most 64 MiB of HBM per device.

v0:
```python
import math

import jax
import jax.numpy as jnp
from jax import lax
from jax.sharding import PartitionSpec as P

D = 1024
HID = 384


learn_rate = 1.0


def soften(latent, fan_in):
    row_scale = jnp.mean(jnp.abs(latent), axis=-1, keepdims=True) + 1e-06
    normed = latent / row_scale
    lower = jnp.tanh(4.0 * (normed - 0.5))
    upper = jnp.tanh(4.0 * (normed + 0.5))
    fan_root = 1.0 / math.sqrt(fan_in)
    weight = (row_scale * 0.5 * (lower + upper) * fan_root).astype(jnp.bfloat16)
    slope = 2.0 * (2.0 - lower * lower - upper * upper) * fan_root
    return (weight, slope)


def dispatch_rows(outbox):
    return lax.all_to_all(outbox, ("inner", "outer"), split_axis=0, concat_axis=0, tiled=True)


def combine_rows(outbox):
    return lax.all_to_all(outbox, ("inner", "outer"), split_axis=0, concat_axis=0, tiled=True)


def upstream_rows(outbox):
    return lax.all_to_all(outbox, ("inner", "outer"), split_axis=0, concat_axis=0, tiled=True)


def on_device(tokens, teacher, expert_ids, gate_codes, gate_up_latent, down_latent):
    experts = lax.axis_size("inner") * lax.axis_size("outer")
    tok_rows, top_count = expert_ids.shape
    part_width = tokens.shape[1]
    capacity = min(tok_rows, 2 * tok_rows * top_count // experts)
    flat_ids = expert_ids.reshape(-1)
    one_hot = (flat_ids[:, None] == jnp.arange(experts, dtype=jnp.int32)[None, :]).astype(jnp.int32)
    before = jnp.cumsum(one_hot, axis=0) - one_hot
    route_slot = jnp.sum(before * one_hot, axis=1)
    target = flat_ids * capacity + route_slot
    payload = jnp.repeat(tokens, top_count, axis=0)
    outbox = jnp.zeros((experts * capacity, part_width), jnp.bfloat16).at[target].set(payload)
    received = dispatch_rows(outbox)
    expert_rows = lax.all_gather(received, "rep", axis=1, tiled=True)
    gu_weight, gu_slope = soften(gate_up_latent[0], D)
    dn_weight, dn_slope = soften(down_latent[0], HID)
    projected = lax.dot_general(
        gu_weight, expert_rows, (((2,), (1,)), ((), ())), preferred_element_type=jnp.float32
    )
    pre_gate = projected[0]
    pre_up = projected[1]
    sigmoid_gate = jax.nn.sigmoid(pre_gate)
    activated = pre_gate * sigmoid_gate
    hidden = (activated * pre_up).astype(jnp.bfloat16)
    partial_out = lax.dot_general(
        hidden, dn_weight, (((0,), (0,)), ((), ())), preferred_element_type=jnp.float32
    )
    expert_out = lax.psum_scatter(
        partial_out.astype(jnp.bfloat16), "rep", scatter_dimension=1, tiled=True
    )
    returned = combine_rows(expert_out)
    picked = returned[target].reshape(tok_rows, top_count, part_width)
    gating = gate_codes.astype(jnp.float32) / 65536.0
    mixed = jnp.sum(gating[:, :, None] * picked.astype(jnp.float32), axis=1)
    student_out = mixed.astype(jnp.bfloat16)
    residual = mixed - teacher.astype(jnp.float32)
    pair_grad = (
        (gating[:, :, None] * residual[:, None, :]).astype(jnp.bfloat16).reshape(-1, part_width)
    )
    grad_outbox = (
        jnp.zeros((experts * capacity, part_width), jnp.bfloat16).at[target].set(pair_grad)
    )
    grad_part = upstream_rows(grad_outbox)
    out_grad = lax.all_gather(grad_part, "rep", axis=1, tiled=True)
    down_grad = jnp.dot(hidden, out_grad, preferred_element_type=jnp.float32)
    hidden_grad = lax.dot_general(
        dn_weight, out_grad, (((1,), (1,)), ((), ())), preferred_element_type=jnp.float32
    )
    gate_grad = (
        hidden_grad * pre_up * sigmoid_gate * (1.0 + pre_gate * (1.0 - sigmoid_gate))
    ).astype(jnp.bfloat16)
    up_grad = (hidden_grad * activated).astype(jnp.bfloat16)
    weight_grads = lax.dot_general(
        jnp.stack([gate_grad, up_grad]),
        expert_rows,
        (((2,), (0,)), ((), ())),
        preferred_element_type=jnp.float32,
    )
    new_gate_up = gate_up_latent - learn_rate * (gu_slope * weight_grads)[None]
    new_down = down_latent - learn_rate * (dn_slope * down_grad)[None]
    return (student_out, new_gate_up, new_down)


def solution(mesh):
    return jax.shard_map(
        on_device,
        mesh=mesh,
        in_specs=(
            P(("parts", "inner", "outer"), "rep"),
            P(("parts", "inner", "outer"), "rep"),
            P(("parts", "inner", "outer"), None),
            P(("parts", "inner", "outer"), None),
            P(("inner", "outer"), None, "rep", None),
            P(("inner", "outer"), "rep", None),
        ),
        out_specs=(
            P(("parts", "inner", "outer"), "rep"),
            P(("parts", "inner", "outer"), None, "rep", None),
            P(("parts", "inner", "outer"), "rep", None),
        ),
        check_vma=False,
    )
```

profile of v0, /device:TPU:0, one launch (start us, length us, event | category | flops | bytes accessed | tf_op | source)
XLA Modules:
  0.0 85.8 jit_solution(5057384777320037804)
XLA Ops:
  7.2 0.8 broadcast_multiply_fusion
  8.0 0.8 copy.12
  9.1 0.6 reduce-window.6
  9.7 0.2 slice_reduce_fusion
  10.0 2.2 %scatter_custom_fusion = bf16[256,512]{1,0:T(8,128)(2,1)} fusion(s32[256]{0:T(256)S(1)} %bitcast.118, bf16[32,512]{1,0:T(8,128)(2,1)S(1)} %copy-done, bf16[]{:T(256)} %constant.12.clone.1), kind=kCustom, calls=%fused_computation.31 | custom fusion | bytes 294914 | tf_op jit(solution)/shard_map/scatter | solution.py:49
  12.2 7.3 %all-to-all-start = ((bf16[8,32,512]{2,1,0:T(8,128)(2,1)}), bf16[8,32,512]{2,1,0:T(8,128)(2,1)S(1)}, u32[]{:S(2)}, u32[]{:S(2)}) async-start(bf16[8,32,512]{2,1,0:T(8,128)(2,1)} %bitcast.6), calls=%async_computation | async-start | bytes 524288 | tf_op jit(solution)/shard_map/all_to_all | solution.py:27
  19.5 1.7 %fusion = f32[2,192]{1,0:T(2,128)S(1)} fusion(f32[1,2,192,1024]{3,2,1,0:T(8,128)} %param.10), kind=kLoop, calls=%fused_computation.6 | loop fusion | flops 786048 | bytes 1574400 | tf_op jit(solution)/shard_map/reduce_sum | solution.py:16
  21.4 7.0 %all-to-all-done = bf16[8,32,512]{2,1,0:T(8,128)(2,1)S(1)} async-done(((bf16[8,32,512]{2,1,0:T(8,128)(2,1)}), bf16[8,32,512]{2,1,0:T(8,128)(2,1)S(1)}, u32[]{:S(2)}, u32[]{:S(2)}) %all-to-all-start) | async-done | bytes 262176 | tf_op jit(solution)/shard_map/all_to_all | solution.py:27
  28.4 2.2 %all_gather.6 = bf16[256,1024]{1,0:T(8,128)(2,1)S(1)} all-gather(bf16[256,512]{1,0:T(8,128)(2,1)S(1)} %bitcast.114), channel_id=1, replica_groups=mesh['parts'=2,'inner'=4,'outer'=2,'rep'=2] {'rep'}, dimensions={1}, use_global_device_ids=true | all-gather | bytes 786432 | tf_op jit(solution)/shard_map/all_gather | solution.py:51
  30.5 0.7 fusion.4
  31.3 0.7 copy-done.5
  32.0 1.4 %convolution_convert_fusion = bf16[256,1024]{1,0:T(8,128)(2,1)} fusion(f32[1,192,1024]{2,1,0:T(8,128)S(1)} %copy-done.2, f32[192]{0:T(256)S(1)} %get-tuple-element.10, f32[192]{0:T(256)S(1)} %get-tuple-element.9, f32[2,192,256]{2,1,0:T(8,128)S(1)} %fusion.4), kind=kOutput, calls=%fused_computation.10 | convolution fusion | flops 102989824 | bytes 1705472 | tf_op jit(solution)/shard_map/dot_general | solution.py:62
  33.5 7.2 %reduce-scatter.2.cloned.1.call-done = bf16[256,512]{1,0:T(8,128)(2,1)} async-done(((bf16[256,1024]{1,0:T(8,128)(2,1)}), bf16[256,512]{1,0:T(8,128)(2,1)}) %reduce-scatter.2.cloned.1.call-update) | async-done | bytes 262160 | tf_op jit(solution)/shard_map/reduce_scatter | solution.py:65
  40.6 5.9 %all-to-all-start.1 = ((bf16[8,32,512]{2,1,0:T(8,128)(2,1)}), bf16[8,32,512]{2,1,0:T(8,128)(2,1)S(1)}, u32[]{:S(2)}, u32[]{:S(2)}) async-start(bf16[8,32,512]{2,1,0:T(8,128)(2,1)} %bitcast.117), calls=%async_computation.2 | async-start | bytes 524288 | tf_op jit(solution)/shard_map/all_to_all | solution.py:31
  46.7 9.2 %all-to-all-done.1 = bf16[8,32,512]{2,1,0:T(8,128)(2,1)S(1)} async-done(((bf16[8,32,512]{2,1,0:T(8,128)(2,1)}), bf16[8,32,512]{2,1,0:T(8,128)(2,1)S(1)}, u32[]{:S(2)}, u32[]{:S(2)}) %all-to-all-start.1) | async-done | bytes 262176 | tf_op jit(solution)/shard_map/all_to_all | solution.py:31
  55.9 1.2 %gather_fusion = bf16[256,512]{1,0:T(8,128)(2,1)S(1)} fusion(bf16[256,512]{1,0:T(8,128)(2,1)S(1)} %bitcast.113, s32[1024]{0:T(1024)S(1)} %pad_clamp_fusion), kind=kCustom, calls=%fused_computation | custom fusion | bytes 525312 | tf_op jit(solution)/shard_map/gather | solution.py:69
  57.0 0.2 fusion.5
  57.3 0.6 convert_subtract_fusion
  57.9 1.6 %scatter_custom_fusion.1 = bf16[256,512]{1,0:T(8,128)(2,1)S(1)} fusion(s32[256]{0:T(256)S(1)} %bitcast.120, f32[32,512]{1,0:T(8,128)S(1)} %get-tuple-element.5, f32[256]{0:T(256)S(1)} %mul.203, bf16[]{:T(256)} %constant.12.clone.1), kind=kCustom, calls=%fused_computation.30 | custom fusion | flops 262144 | bytes 328706 | tf_op jit(solution)/shard_map/scatter | solution.py:78
  59.5 12.3 %all_to_all.36 = bf16[8,32,512]{2,1,0:T(8,128)(2,1)S(1)} all-to-all(bf16[8,32,512]{2,1,0:T(8,128)(2,1)S(1)} %bitcast.116), channel_id=1, replica_groups=mesh['parts'=2,'inner'=4,'outer'=2,'rep'=2] {'inner','outer'}, dimensions={0} | all-to-all | bytes 524288 | tf_op jit(solution)/shard_map/all_to_all | solution.py:35
  71.9 2.2 %all_gather.7 = bf16[256,1024]{1,0:T(8,128)(2,1)S(1)} all-gather(bf16[256,512]{1,0:T(8,128)(2,1)S(1)} %bitcast.115), channel_id=1, replica_groups=mesh['parts'=2,'inner'=4,'outer'=2,'rep'=2] {'rep'}, dimensions={1}, use_global_device_ids=true | all-gather | bytes 786432 | tf_op jit(solution)/shard_map/all_gather | solution.py:81
  74.0 1.6 %fusion.34 = (bf16[1,192,256]{2,1,0:T(8,128)(2,1)S(1)}, bf16[1,192,256]{2,1,0:T(8,128)(2,1)S(1)}) fusion(f32[2,192,256]{2,1,0:T(8,128)} %copy-done.5, bf16[256,1024]{1,0:T(8,128)(2,1)S(1)} %all_gather.7, f32[1,192,1024]{2,1,0:T(8,128)S(1)} %copy-done.2, f32[192]{0:T(256)S(1)} %get-tuple-element.10, f32[192]{0:T(256)S(1)} %get-tuple-element.9), kind=kOutput, calls=%fused_computation.58 | convolution fusion | flops 103071744 | bytes 1902080 | tf_op jit(solution)/shard_map/dot_general | solution.py:83
  75.6 1.4 %fusion.2 = f32[1,192,1024]{2,1,0:T(8,128)} fusion(f32[1,192,1024]{2,1,0:T(8,128)S(1)} %copy-done.2, bf16[256,1024]{1,0:T(8,128)(2,1)S(1)} %all_gather.7, f32[192]{0:T(256)S(1)} %get-tuple-element.10, f32[2,192,256]{2,1,0:T(8,128)S(1)} %copy-done.6), kind=kOutput, calls=%fused_computation.13 | convolution fusion | flops 103317504 | bytes 2491136 | tf_op jit(solution)/shard_map/dot_general | solution.py:82
  77.0 2.0 %bitcast_subtract_fusion = f32[1,2,192,1024]{3,2,1,0:T(8,128)} fusion(f32[1,2,192,1024]{3,2,1,0:T(8,128)S(1)} %copy-done.1, f32[2,192]{1,0:T(2,128)S(1)} %get-tuple-element.8, bf16[256,1024]{1,0:T(8,128)(2,1)S(1)} %all_gather.6, bf16[1,192,256]{2,1,0:T(8,128)(2,1)S(1)} %get-tuple-element.4, bf16[1,192,256]{2,1,0:T(8,128)(2,1)S(1)} %get-tuple-element.3), kind=kOutput, calls=%fused_computation.3 | convolution fusion | flops 206143488 | bytes 3868160 | tf_op jit(solution)/shard_map/dot_general | solution.py:90
  (31 shorter events, 0.9 us)
Async XLA Ops:
  7.2 2.9 %copy-start = (bf16[32,512]{1,0:T(8,128)(2,1)S(1)}, bf16[32,512]{1,0:T(8,128)(2,1)}, u32[]{:S(2)}) copy-start(bf16[32,512]{1,0:T(8,128)(2,1)} %param.6) | copy-start | bytes 98308
  7.2 14.1 %copy-start.2 = (f32[1,192,1024]{2,1,0:T(8,128)S(1)}, f32[1,192,1024]{2,1,0:T(8,128)}, u32[]{:S(2)}) copy-start(f32[1,192,1024]{2,1,0:T(8,128)} %param.11) | copy-start | bytes 2359300
  12.2 16.2 %all-to-all-start = ((bf16[8,32,512]{2,1,0:T(8,128)(2,1)}), bf16[8,32,512]{2,1,0:T(8,128)(2,1)S(1)}, u32[]{:S(2)}, u32[]{:S(2)}) async-start(bf16[8,32,512]{2,1,0:T(8,128)(2,1)} %bitcast.6), calls=%async_computation | async-start | bytes 524288 | tf_op jit(solution)/shard_map/all_to_all | solution.py:27
  19.5 11.1 %copy-start.1 = (f32[1,2,192,1024]{3,2,1,0:T(8,128)S(1)}, f32[1,2,192,1024]{3,2,1,0:T(8,128)}, u32[]{:S(2)}) copy-start(f32[1,2,192,1024]{3,2,1,0:T(8,128)} %param.10) | copy-start | bytes 4718596
  19.5 21.1 %reduce-scatter.2.cloned.1.call-start = ((), (), s32[]{:S(2)}) async-start(), calls=%async_computation.4 | async-start | bytes 786432 | tf_op jit(solution)/shard_map/reduce_scatter | solution.py:65
  31.3 0.7 copy-start.5
  32.0 14.4 %copy-start.4 = (s32[32,8]{0,1:T(8,128)S(1)}, s32[32,8]{0,1:T(8,128)}, u32[]{:S(2)}) copy-start(s32[32,8]{0,1:T(8,128)} %param.9) | copy-start | bytes 3076
  40.6 16.6 %copy-start.3 = (bf16[32,512]{1,0:T(8,128)(2,1)S(1)}, bf16[32,512]{1,0:T(8,128)(2,1)}, u32[]{:S(2)}) copy-start(bf16[32,512]{1,0:T(8,128)(2,1)} %param.7) | copy-start | bytes 98308
  40.6 15.3 %all-to-all-start.1 = ((bf16[8,32,512]{2,1,0:T(8,128)(2,1)}), bf16[8,32,512]{2,1,0:T(8,128)(2,1)S(1)}, u32[]{:S(2)}, u32[]{:S(2)}) async-start(bf16[8,32,512]{2,1,0:T(8,128)(2,1)} %bitcast.117), calls=%async_computation.2 | async-start | bytes 524288 | tf_op jit(solution)/shard_map/all_to_all | solution.py:31
  74.0 1.6 %copy-start.6 = (f32[2,192,256]{2,1,0:T(8,128)S(1)}, f32[2,192,256]{2,1,0:T(8,128)}, u32[]{:S(2)}) copy-start(f32[2,192,256]{2,1,0:T(8,128)} %copy-done.5) | copy-start | bytes 1179652
Sparse Core Ops, SparseCore 0:
  33.6 6.9 reduce-scatter.1
where the time goes:
time: 86.3 us; the launch traced here: 85.8 us
  waiting for transfers between devices  23.3 us (27%)
  blocking collectives  16.7 us (19%)
  between operations  14.2 us (16%)
  starting transfers between devices  13.2 us (15%)
  matrix products  7.07 us (8%)
  other arithmetic  5.84 us (7%)
  local copies, waits for them, and re-layouts  5.57 us (6%)
    all_to_all x1, blocking collectives, upstream_rows(): lax.all_to_all(outbox, ('inner', 'outer'), split_axis=0, concat_axis=0, t...  12.3 us
    all_to_all x1, waiting for transfers between devices, combine_rows(): lax.all_to_all(outbox, ('inner', 'outer'), split_axis=0, concat_axis=0, t...  9.19 us
    all_to_all x1, starting transfers between devices, dispatch_rows(): lax.all_to_all(outbox, ('inner', 'outer'), split_axis=0, concat_axis=0, t...  7.25 us
    reduce_scatter x1, waiting for transfers between devices, on_device(): lax.psum_scatter(partial_out.astype(jnp.bfloat16), 'rep', scatter_dimensi...  7.15 us
    all_to_all x1, waiting for transfers between devices, dispatch_rows(): lax.all_to_all(outbox, ('inner', 'outer'), split_axis=0, concat_axis=0, t...  6.97 us
    all_to_all x1, starting transfers between devices, combine_rows(): lax.all_to_all(outbox, ('inner', 'outer'), split_axis=0, concat_axis=0, t...  5.88 us
    all_gather x1, blocking collectives, on_device(): expert_rows = lax.all_gather(received, 'rep', axis=1, tiled=True)  2.17 us
    all_gather x1, blocking collectives, on_device(): out_grad = lax.all_gather(grad_part, 'rep', axis=1, tiled=True)  2.17 us
  transfers between devices with their start and end apart: 3, of which 3 were waited for; matrix products, arithmetic and copies ran while one was open for 2% of the time, Pallas kernels for 0%

commit v1 on v0

--- a/solution.py
+++ b/solution.py
@@ -1,8 +1,11 @@
+import functools
 import math
 
 import jax
 import jax.numpy as jnp
 from jax import lax
+from jax.experimental import pallas as pl
+from jax.experimental.pallas import tpu as pltpu
 from jax.sharding import PartitionSpec as P
 
 D = 1024
@@ -35,7 +38,7 @@
     return lax.all_to_all(outbox, ("inner", "outer"), split_axis=0, concat_axis=0, tiled=True)
 
 
-def on_device(tokens, teacher, expert_ids, gate_codes, gate_up_latent, down_latent):
+def routed_step(tokens, teacher, expert_ids, gate_codes, gate_up_latent, down_latent):
     experts = lax.axis_size("inner") * lax.axis_size("outer")
     tok_rows, top_count = expert_ids.shape
     part_width = tokens.shape[1]
@@ -96,6 +99,335 @@
     new_gate_up = gate_up_latent - learn_rate * (gu_slope * weight_grads)[None]
     new_down = down_latent - learn_rate * (dn_slope * down_grad)[None]
     return (student_out, new_gate_up, new_down)
+
+
+MESH = pl.DeviceIdType.MESH
+LANES = 128
+BF16 = jnp.bfloat16
+F32 = jnp.float32
+
+
+def dot_t(a, b):
+    return lax.dot_general(a, b, (((1,), (1,)), ((), ())), preferred_element_type=F32)
+
+
+def dense_kernel(
+    n_inner, n_outer,
+    tokens_ref, teacher_ref, ids_ref, codes_ref, gu_ref, dn_ref,
+    student_ref, new_gu_ref, new_dn_ref,
+    rows, resid, resid_own, gates_own, gates, latent, weight, slope,
+    gated_hidden, factor, half_out, half_in, mine, sums, returned,
+    load_sem, store_sem, gate_send, gate_recv, tok_send, tok_recv, tok_rep,
+    half_send, half_recv, sum_send, sum_recv, res_send, res_recv, res_rep,
+):
+    n = n_inner * n_outer
+    tok_rows, width = tokens_ref.shape
+    hid = latent.shape[1]
+    inner, outer, rep = lax.axis_index("inner"), lax.axis_index("outer"), lax.axis_index("rep")
+    me = inner * n_outer + outer
+    partner = {"rep": 1 - rep}
+
+    def inner_at(step):
+        return lax.rem(inner + step + n_inner, n_inner)
+
+    def outer_at(step):
+        return lax.rem(outer + step + n_outer, n_outer)
+
+    def peer_at(step):
+        peer = lax.rem(me + step + n, n)
+        return peer, {"inner": peer // n_outer, "outer": lax.rem(peer, n_outer)}
+
+    def remote(source, target, send, recv, device):
+        return pltpu.make_async_remote_copy(
+            src_ref=source, dst_ref=target, send_sem=send, recv_sem=recv,
+            device_id=device, device_id_type=MESH,
+        )
+
+    loads = [
+        pltpu.make_async_copy(gu_ref.at[0, 0], latent.at[0], load_sem.at[0]),
+        pltpu.make_async_copy(gu_ref.at[0, 1], latent.at[1], load_sem.at[1]),
+        pltpu.make_async_copy(dn_ref.at[0], latent.at[2], load_sem.at[2]),
+    ]
+    for load in loads:
+        load.start()
+
+    barrier = pltpu.get_barrier_semaphore()
+    pl.semaphore_signal(barrier, inc=1, device_id=partner, device_id_type=MESH)
+    for step in range(1, n):
+        pl.semaphore_signal(barrier, inc=1, device_id=peer_at(step)[1], device_id_type=MESH)
+    pl.semaphore_wait(barrier, n)
+
+    def gather_start(own, buf, send, recv, rep_recv):
+        sent = []
+
+        def push(source, slot, sem, device):
+            copy = remote(source, buf.at[rep, slot], send.at[len(sent)], sem, device)
+            copy.start()
+            sent.append(copy)
+
+        for step in range(1, n_inner):
+            push(own, me, recv.at[me], {"inner": inner_at(step)})
+        for step in range(1, n_outer):
+            push(own, me, recv.at[me], {"outer": outer_at(step)})
+        push(own, me, rep_recv.at[me], partner)
+        buf[rep, me] = own[...]
+        return sent, push
+
+    def gather_rest(own, buf, send, recv, rep_recv, sent, push, between):
+        def arrived(slot):
+            remote(own, buf.at[rep, slot], send.at[0], recv.at[slot], partner).wait_recv()
+
+        for step in range(1, n_inner):
+            slot = inner_at(-step) * n_outer + outer
+            arrived(slot)
+            for across in range(1, n_outer):
+                push(buf.at[rep, slot], slot, recv.at[slot], {"outer": outer_at(across)})
+            push(buf.at[rep, slot], slot, rep_recv.at[slot], partner)
+            between()
+        for step in range(n_inner):
+            for across in range(1, n_outer):
+                slot = inner_at(-step) * n_outer + outer_at(-across)
+                arrived(slot)
+                push(buf.at[rep, slot], slot, rep_recv.at[slot], partner)
+            between()
+        for slot in range(n):
+            remote(own, buf.at[1 - rep, slot], send.at[0], rep_recv.at[slot], partner).wait_recv()
+        for copy in sent:
+            copy.wait_send()
+
+    tok_sent, tok_push = gather_start(tokens_ref, rows, tok_send, tok_recv, tok_rep)
+
+    ids = ids_ref[...]
+    gate_of = codes_ref[...].astype(F32) * (1.0 / 65536.0)
+    lane = lax.broadcasted_iota(jnp.int32, (LANES, LANES), 1)
+    table = jnp.zeros((LANES, LANES), F32)
+    for expert in range(n):
+        column = jnp.sum(jnp.where(ids == expert, gate_of, 0.0), axis=1, keepdims=True)
+        column = jnp.concatenate([column, jnp.zeros((LANES - tok_rows, 1), F32)], axis=0)
+        table = jnp.where(lane == expert, column, table)
+    gates_own[...] = table.T[: gates_own.shape[0]]
+    gate_sent = []
+    for step in range(1, n):
+        copy = remote(
+            gates_own, gates.at[me], gate_send.at[step - 1], gate_recv.at[me], peer_at(step)[1]
+        )
+        copy.start()
+        gate_sent.append(copy)
+    gates[me] = gates_own[...]
+
+    fan_root = [1.0 / math.sqrt(latent.shape[2])] * 2 + [1.0 / math.sqrt(2 * hid)]
+    piece = 32
+
+    def soften_rows(matrix, first, last):
+        root = fan_root[matrix]
+
+        def body(at, carry):
+            part = pl.ds(pl.multiple_of(at * piece, piece), piece)
+            value = latent[matrix, part, :]
+            row_scale = jnp.mean(jnp.abs(value), axis=-1, keepdims=True) + 1e-06
+            normed = value / row_scale
+            lower = jnp.tanh(4.0 * (normed - 0.5))
+            upper = jnp.tanh(4.0 * (normed + 0.5))
+            weight[matrix, part, :] = (row_scale * (0.5 * root) * (lower + upper)).astype(BF16)
+            slope[matrix, part, :] = (2.0 * root) * (2.0 - lower * lower - upper * upper)
+            return carry
+
+        lax.fori_loop(first, last, body, 0)
+
+    half = hid // piece // 2
+    work = [(m, a, b) for m in range(3) for a, b in ((0, half), (half, hid // piece))]
+
+    def soften_next():
+        if work:
+            matrix, first, last = work.pop(0)
+            if first == 0:
+                loads[matrix].wait()
+            soften_rows(matrix, first, last)
+
+    soften_next()
+    gather_rest(
+        tokens_ref, rows, tok_send, tok_recv, tok_rep, tok_sent, tok_push, soften_next
+    )
+    while work:
+        soften_next()
+
+    for step in range(1, n):
+        slot = peer_at(-step)[0]
+        remote(gates_own, gates.at[slot], gate_send.at[0], gate_recv.at[slot], partner).wait_recv()
+    for copy in gate_sent:
+        copy.wait_send()
+    spread = LANES // tok_rows
+    gate_row = jnp.concatenate(
+        [
+            sum(
+                pltpu.roll(gates[base + at, pl.ds(me, 1), :], at * tok_rows, 1) if at
+                else gates[base, pl.ds(me, 1), :]
+                for at in range(spread)
+            )
+            for base in range(0, n, spread)
+        ],
+        axis=1,
+    )
+
+    def flat(ref, index):
+        return ref[index].reshape(n * tok_rows, width)
+
+    both = weight[0:2].reshape(2 * hid, 2 * width)
+    pre = dot_t(both[:, :width], flat(rows, 0)) + dot_t(both[:, width:], flat(rows, 1))
+    pre_gate, pre_up = pre[:hid], pre[hid:]
+    sigmoid_gate = jax.nn.sigmoid(pre_gate)
+    activated = pre_gate * sigmoid_gate
+    hidden = activated * pre_up * gate_row
+    gated_hidden[...] = hidden.astype(BF16)
+    hidden_t = hidden.T.astype(BF16)
+
+    other_cols = pl.ds(pl.multiple_of((1 - rep) * width, width), width)
+    own_cols = pl.ds(pl.multiple_of(rep * width, width), width)
+    half_out[...] = (
+        jnp.dot(hidden_t, weight[2, :, other_cols], preferred_element_type=F32)
+        .astype(BF16).reshape(n, tok_rows, width)
+    )
+    order = [peer_at(step) for step in range(1, n)] + [(me, None)]
+    half_sent = []
+    for slot, _ in order:
+        copy = remote(half_out.at[slot], half_in.at[slot], half_send.at[slot], half_recv.at[slot], partner)
+        copy.start()
+        half_sent.append(copy)
+    mine[...] = jnp.dot(
+        hidden_t, weight[2, :, own_cols], preferred_element_type=F32
+    ).reshape(n, tok_rows, width)
+
+    sum_sent = []
+    for at, (slot, device) in enumerate(order):
+        half_sent[at].wait_recv()
+        total = mine[slot] + half_in[slot].astype(F32)
+        if device is None:
+            mine[slot] = total
+        else:
+            sums[slot] = total.astype(BF16)
+            copy = remote(
+                sums.at[slot], returned.at[me], sum_send.at[at], sum_recv.at[me], device
+            )
+            copy.start()
+            sum_sent.append(copy)
+
+    factor[0] = gate_row * pre_up * sigmoid_gate * (1.0 + pre_gate * (1.0 - sigmoid_gate))
+    factor[1] = gate_row * activated
+
+    mixed = mine[me]
+    for step in range(1, n):
+        slot = peer_at(-step)[0]
+        remote(resid_own, returned.at[slot], sum_send.at[0], sum_recv.at[slot], partner).wait_recv()
+        mixed = mixed + returned[slot].astype(F32)
+    student_ref[...] = mixed.astype(BF16)
+    resid_own[...] = (mixed - teacher_ref[...].astype(F32)).astype(BF16)
+
+    res_sent, res_push = gather_start(resid_own, resid, res_send, res_recv, res_rep)
+    gather_rest(
+        resid_own, resid, res_send, res_recv, res_rep, res_sent, res_push, lambda: None
+    )
+    for copy in half_sent + sum_sent:
+        copy.wait_send()
+
+    down = weight[2]
+    hidden_grad = dot_t(down[:, :width], flat(resid, 0)) + dot_t(down[:, width:], flat(resid, 1))
+    grads = [
+        (hidden_grad * factor[0]).astype(BF16),
+        (hidden_grad * factor[1]).astype(BF16),
+        gated_hidden[...],
+    ]
+    targets = [new_gu_ref.at[0, 0], new_gu_ref.at[0, 1], new_dn_ref.at[0]]
+    tile = min(width, 256)
+    stores = []
+    for matrix in (2, 0, 1):
+        source = resid if matrix == 2 else rows
+        for side in range(2):
+            for first in range(0, width, tile):
+                block = source[side, :, :, first : first + tile].reshape(n * tok_rows, tile)
+                grad = jnp.dot(grads[matrix], block, preferred_element_type=F32)
+                cols = slice(side * width + first, side * width + first + tile)
+                slope[matrix, :, cols] = latent[matrix, :, cols] - learn_rate * (
+                    slope[matrix, :, cols] * grad
+                )
+        store = pltpu.make_async_copy(slope.at[matrix], targets[matrix], store_sem.at[matrix])
+        store.start()
+        stores.append(store)
+    for store in stores:
+        store.wait()
+
+
+def dense_step(tokens, teacher, expert_ids, gate_codes, gate_up_latent, down_latent):
+    n_inner, n_outer = lax.axis_size("inner"), lax.axis_size("outer")
+    n = n_inner * n_outer
+    tok_rows, width = tokens.shape
+    hid, full = down_latent.shape[1:]
+    sublanes = -(-n // 8) * 8
+    gather_sends = (n_inner - 1) * (1 + n_outer) + (n_outer - 1) * (1 + n_inner) + 1
+    dma = pltpu.SemaphoreType.DMA
+    block = (n, tok_rows, width)
+    vmem = pl.BlockSpec(memory_space=pltpu.VMEM)
+    hbm = pl.BlockSpec(memory_space=pl.ANY)
+    return pl.pallas_call(
+        functools.partial(dense_kernel, n_inner, n_outer),
+        out_shape=(
+            jax.ShapeDtypeStruct(tokens.shape, BF16),
+            jax.ShapeDtypeStruct(gate_up_latent.shape, F32),
+            jax.ShapeDtypeStruct(down_latent.shape, F32),
+        ),
+        in_specs=[vmem, vmem, vmem, vmem, hbm, hbm],
+        out_specs=(vmem, hbm, hbm),
+        scratch_shapes=[
+            pltpu.VMEM((2, *block), BF16),
+            pltpu.VMEM((2, *block), BF16),
+            pltpu.VMEM((tok_rows, width), BF16),
+            pltpu.VMEM((sublanes, LANES), F32),
+            pltpu.VMEM((n, sublanes, LANES), F32),
+            pltpu.VMEM((3, hid, full), F32),
+            pltpu.VMEM((3, hid, full), BF16),
+            pltpu.VMEM((3, hid, full), F32),
+            pltpu.VMEM((hid, n * tok_rows), BF16),
+            pltpu.VMEM((2, hid, n * tok_rows), F32),
+            pltpu.VMEM(block, BF16),
+            pltpu.VMEM(block, BF16),
+            pltpu.VMEM(block, F32),
+            pltpu.VMEM(block, BF16),
+            pltpu.VMEM(block, BF16),
+            dma((3,)),
+            dma((3,)),
+            dma((n,)),
+            dma((n,)),
+            dma((gather_sends,)),
+            dma((n,)),
+            dma((n,)),
+            dma((n,)),
+            dma((n,)),
+            dma((n,)),
+            dma((n,)),
+            dma((gather_sends,)),
+            dma((n,)),
+            dma((n,)),
+        ],
+        compiler_params=pltpu.CompilerParams(
+            collective_id=0, has_side_effects=True, vmem_limit_bytes=40 * 1024 * 1024
+        ),
+    )(tokens, teacher, expert_ids, gate_codes, gate_up_latent, down_latent)
+
+
+def on_device(tokens, teacher, expert_ids, gate_codes, gate_up_latent, down_latent):
+    experts = lax.axis_size("inner") * lax.axis_size("outer")
+    tok_rows, top_count = expert_ids.shape
+    whole_block = 2 * top_count >= experts
+    fits = (
+        lax.axis_size("rep") == 2
+        and LANES % tok_rows == 0
+        and tok_rows % 16 == 0
+        and experts <= LANES
+        and experts * tok_rows % LANES == 0
+        and tokens.shape[1] % LANES == 0
+        and down_latent.shape[1] % 64 == 0
+    )
+    step = dense_step if whole_block and fits else routed_step
+    return step(tokens, teacher, expert_ids, gate_codes, gate_up_latent, down_latent)
 
 
 def solution(mesh):

time: 86.3 us -> 44.1 us (0.51)
  Pallas kernels: 0 us -> 34.8 us
  waiting for transfers between devices: 23.3 us -> 0 us
  blocking collectives: 16.7 us -> 0 us
  between operations: 14.2 us -> 0.64 us
  starting transfers between devices: 13.2 us -> 0 us
  matrix products: 7.07 us -> 0 us
  other arithmetic: 5.84 us -> 0 us
  local copies, waits for them, and re-layouts: 5.57 us -> 8.22 us
    pallas_call x0 -> x1, Pallas kernels: none -> 34.8 us  [dense_step(): pl.pallas_call(functools.partial(dense_kernel, n_inner, n_outer), out_sha...]
    all_to_all x2 -> x0, waiting for transfers between devices: 16.2 us -> none  [the longest x1 9.19 us: combine_rows(): lax.all_to_all(outbox, ('inner', 'outer'), split_axis=0, concat_axis=0, t...]
    all_to_all x2 -> x0, starting transfers between devices: 13.1 us -> none  [the longest x1 7.25 us: dispatch_rows(): lax.all_to_all(outbox, ('inner', 'outer'), split_axis=0, concat_axis=0, t...]
    all_to_all x1 -> x0, blocking collectives: 12.3 us -> none  [upstream_rows(): lax.all_to_all(outbox, ('inner', 'outer'), split_axis=0, concat_axis=0, t...]
    reduce_scatter x1 -> x0, waiting for transfers between devices: 7.15 us -> none  [on_device(): lax.psum_scatter(partial_out.astype(jnp.bfloat16), 'rep', scatter_dimensi...]
    dot_general x5 -> x0, matrix products: 7.07 us -> none  [the longest x1 2 us: on_device(): lax.dot_general(jnp.stack([gate_grad, up_grad]), expert_rows, (((2,), (0,...]
    unnamed x15 -> x13, local copies, waits for them, and re-layouts: 1.53 us -> 8.22 us
    all_gather x2 -> x0, blocking collectives: 4.34 us -> none  [the longest x1 2.17 us: on_device(): expert_rows = lax.all_gather(received, 'rep', axis=1, tiled=True)]
  transfers between devices with their start and end apart: 3 -> 0, of which waited for: 3 -> 0; matrix products, arithmetic and copies ran while one was open for 2% -> 0% of each run, Pallas kernels for 0% -> 0%
where the time goes in v1:
time: 44.1 us; the launch traced here: 43.7 us
  Pallas kernels  34.8 us (79%)
  local copies, waits for them, and re-layouts  8.22 us (19%)
  between operations  0.64 us (1%)
    pallas_call x1, Pallas kernels, dense_step(): pl.pallas_call(functools.partial(dense_kernel, n_inner, n_outer), out_sha...  34.8 us
    unnamed x13, local copies, waits for them, and re-layouts  8.22 us

profile of v1, /device:TPU:0, one launch (start us, length us, event | category | flops | bytes accessed | tf_op | source)
XLA Modules:
  0.0 43.7 jit_solution(13013916791094156147)
XLA Ops:
  0.6 0.8 %copy.9.ids_ref = s32[32,8]{1,0:T(8,128)S(1)} copy(s32[32,8]{0,1:T(8,128)} %param.8) | data formatting | bytes 2048 | tf_op args[2]
  1.4 0.8 %copy.10.codes_ref = s32[32,8]{1,0:T(8,128)S(1)} copy(s32[32,8]{0,1:T(8,128)} %param.9) | data formatting | bytes 2048 | tf_op args[3]
  2.2 0.0 copy-start
  2.2 1.4 %copy-done = f32[1,2,192,1024]{3,2,1,0:T(8,128)S(1)} copy-done((f32[1,2,192,1024]{3,2,1,0:T(8,128)S(1)}, f32[1,2,192,1024]{3,2,1,0:T(8,128)}, u32[]{:S(2)}) %copy-start) | copy-done | bytes 1572888
  3.6 0.0 copy-start.1
  3.6 1.1 %copy-done.1 = f32[1,192,1024]{2,1,0:T(8,128)S(1)} copy-done((f32[1,192,1024]{2,1,0:T(8,128)S(1)}, f32[1,192,1024]{2,1,0:T(8,128)}, u32[]{:S(2)}) %copy-start.1) | copy-done | bytes 786456
  4.7 0.0 copy-start.2
  4.7 0.8 %copy-done.2 = bf16[32,512]{1,0:T(8,128)(2,1)S(1)} copy-done((bf16[32,512]{1,0:T(8,128)(2,1)S(1)}, bf16[32,512]{1,0:T(8,128)(2,1)}, u32[]{:S(2)}) %copy-start.2) | copy-done | bytes 32792
  5.5 0.0 copy-start.3
  5.5 0.8 %copy-done.3 = bf16[32,512]{1,0:T(8,128)(2,1)S(1)} copy-done((bf16[32,512]{1,0:T(8,128)(2,1)S(1)}, bf16[32,512]{1,0:T(8,128)(2,1)}, u32[]{:S(2)}) %copy-start.3) | copy-done | bytes 32792
  6.2 34.8 %shard_map.85 = (bf16[32,512]{1,0:T(8,128)(2,1)S(1)}, f32[1,2,192,1024]{3,2,1,0:T(8,128)S(1)}, f32[1,192,1024]{2,1,0:T(8,128)S(1)}) custom-call(bf16[32,512]{1,0:T(8,128)(2,1)S(1)} %copy-done.2, bf16[32,512]{1,0:T(8,128)(2,1)S(1)} %copy-done.3, s32[32,8]{1,0:T(8,128)S(1)} %copy.9.ids_ref, s32[32,8]{1,0:T(8,128)S(1)} %copy.10.codes_ref, ...), custom_call_target="tpu_custom_call" | custom-call | tf_op jit(solution)/shard_map/pallas_call | solution.py:370
  41.1 0.6 %copy.14 = bf16[32,512]{1,0:T(8,128)(2,1)} copy(bf16[32,512]{1,0:T(8,128)(2,1)S(1)} %get-tuple-element.6) | data formatting | bytes 65536
  41.7 1.1 %copy.15 = f32[1,2,192,1024]{3,2,1,0:T(8,128)} copy(f32[1,2,192,1024]{3,2,1,0:T(8,128)S(1)} %get-tuple-element.7) | data formatting | bytes 3145728
  42.8 0.9 %copy.16 = f32[1,192,1024]{2,1,0:T(8,128)} copy(f32[1,192,1024]{2,1,0:T(8,128)S(1)} %get-tuple-element.8) | data formatting | bytes 1572864
Async XLA Ops:
  2.2 1.4 %copy-start = (f32[1,2,192,1024]{3,2,1,0:T(8,128)S(1)}, f32[1,2,192,1024]{3,2,1,0:T(8,128)}, u32[]{:S(2)}) copy-start(f32[1,2,192,1024]{3,2,1,0:T(8,128)} %gu_ref.1) | copy-start | bytes 4718596
  3.6 1.1 %copy-start.1 = (f32[1,192,1024]{2,1,0:T(8,128)S(1)}, f32[1,192,1024]{2,1,0:T(8,128)}, u32[]{:S(2)}) copy-start(f32[1,192,1024]{2,1,0:T(8,128)} %dn_ref.1) | copy-start | bytes 2359300
  4.7 0.8 %copy-start.2 = (bf16[32,512]{1,0:T(8,128)(2,1)S(1)}, bf16[32,512]{1,0:T(8,128)(2,1)}, u32[]{:S(2)}) copy-start(bf16[32,512]{1,0:T(8,128)(2,1)} %tokens_ref.1) | copy-start | bytes 98308
  5.5 0.8 %copy-start.3 = (bf16[32,512]{1,0:T(8,128)(2,1)S(1)}, bf16[32,512]{1,0:T(8,128)(2,1)}, u32[]{:S(2)}) copy-start(bf16[32,512]{1,0:T(8,128)(2,1)} %teacher_ref.1) | copy-start | bytes 98308

commit v2 on v1

--- a/solution.py
+++ b/solution.py
@@ -114,10 +114,10 @@
 def dense_kernel(
     n_inner, n_outer,
     tokens_ref, teacher_ref, ids_ref, codes_ref, gu_ref, dn_ref,
-    student_ref, new_gu_ref, new_dn_ref,
-    rows, resid, resid_own, gates_own, gates, latent, weight, slope,
-    gated_hidden, factor, half_out, half_in, mine, sums, returned,
-    load_sem, store_sem, gate_send, gate_recv, tok_send, tok_recv, tok_rep,
+    student, grads, rows, resid, latent, slope,
+    teacher, ids, codes, resid_own, gates_own, gates, weight,
+    factor, half_out, half_in, mine, sums, returned,
+    load_sem, gate_send, gate_recv, tok_send, tok_recv, tok_rep,
     half_send, half_recv, sum_send, sum_recv, res_send, res_recv, res_rep,
 ):
     n = n_inner * n_outer
@@ -147,6 +147,10 @@
         pltpu.make_async_copy(gu_ref.at[0, 0], latent.at[0], load_sem.at[0]),
         pltpu.make_async_copy(gu_ref.at[0, 1], latent.at[1], load_sem.at[1]),
         pltpu.make_async_copy(dn_ref.at[0], latent.at[2], load_sem.at[2]),
+        pltpu.make_async_copy(tokens_ref, rows.at[rep, me], load_sem.at[3]),
+        pltpu.make_async_copy(teacher_ref, teacher, load_sem.at[4]),
+        pltpu.make_async_copy(ids_ref, ids, load_sem.at[5]),
+        pltpu.make_async_copy(codes_ref, codes, load_sem.at[6]),
     ]
     for load in loads:
         load.start()
@@ -170,7 +174,6 @@
         for step in range(1, n_outer):
             push(own, me, recv.at[me], {"outer": outer_at(step)})
         push(own, me, rep_recv.at[me], partner)
-        buf[rep, me] = own[...]
         return sent, push
 
     def gather_rest(own, buf, send, recv, rep_recv, sent, push, between):
@@ -192,20 +195,19 @@
             between()
         for slot in range(n):
             remote(own, buf.at[1 - rep, slot], send.at[0], rep_recv.at[slot], partner).wait_recv()
-        for copy in sent:
-            copy.wait_send()
 
     tok_sent, tok_push = gather_start(tokens_ref, rows, tok_send, tok_recv, tok_rep)
 
-    ids = ids_ref[...]
-    gate_of = codes_ref[...].astype(F32) * (1.0 / 65536.0)
-    lane = lax.broadcasted_iota(jnp.int32, (LANES, LANES), 1)
-    table = jnp.zeros((LANES, LANES), F32)
+    loads[5].wait()
+    loads[6].wait()
+    gate_of = codes[...].astype(F32) * (1.0 / 65536.0)
+    line = lax.broadcasted_iota(jnp.int32, (gates_own.shape[0], tok_rows), 0)
+    table = jnp.zeros((gates_own.shape[0], tok_rows), F32)
     for expert in range(n):
-        column = jnp.sum(jnp.where(ids == expert, gate_of, 0.0), axis=1, keepdims=True)
-        column = jnp.concatenate([column, jnp.zeros((LANES - tok_rows, 1), F32)], axis=0)
-        table = jnp.where(lane == expert, column, table)
-    gates_own[...] = table.T[: gates_own.shape[0]]
+        row = jnp.sum(jnp.where(ids[...] == expert, gate_of, 0.0), axis=0, keepdims=True)
+        table = jnp.where(line == expert, row, table)
+    gates_own[...] = jnp.zeros_like(gates_own)
+    gates_own[:, :tok_rows] = table
     gate_sent = []
     for step in range(1, n):
         copy = remote(
@@ -250,12 +252,11 @@
     )
     while work:
         soften_next()
+    loads[3].wait()
 
     for step in range(1, n):
         slot = peer_at(-step)[0]
         remote(gates_own, gates.at[slot], gate_send.at[0], gate_recv.at[slot], partner).wait_recv()
-    for copy in gate_sent:
-        copy.wait_send()
     spread = LANES // tok_rows
     gate_row = jnp.concatenate(
         [
@@ -278,7 +279,7 @@
     sigmoid_gate = jax.nn.sigmoid(pre_gate)
     activated = pre_gate * sigmoid_gate
     hidden = activated * pre_up * gate_row
-    gated_hidden[...] = hidden.astype(BF16)
+    grads[2] = hidden.astype(BF16)
     hidden_t = hidden.T.astype(BF16)
 
     other_cols = pl.ds(pl.multiple_of((1 - rep) * width, width), width)
@@ -319,37 +320,44 @@
         slot = peer_at(-step)[0]
         remote(resid_own, returned.at[slot], sum_send.at[0], sum_recv.at[slot], partner).wait_recv()
         mixed = mixed + returned[slot].astype(F32)
-    student_ref[...] = mixed.astype(BF16)
-    resid_own[...] = (mixed - teacher_ref[...].astype(F32)).astype(BF16)
+    student[...] = mixed.astype(BF16)
+    loads[4].wait()
+    resid_own[...] = (mixed - teacher[...].astype(F32)).astype(BF16)
+    resid[rep, me] = resid_own[...]
 
     res_sent, res_push = gather_start(resid_own, resid, res_send, res_recv, res_rep)
     gather_rest(
         resid_own, resid, res_send, res_recv, res_rep, res_sent, res_push, lambda: None
     )
-    for copy in half_sent + sum_sent:
-        copy.wait_send()
 
     down = weight[2]
     hidden_grad = dot_t(down[:, :width], flat(resid, 0)) + dot_t(down[:, width:], flat(resid, 1))
-    grads = [
-        (hidden_grad * factor[0]).astype(BF16),
-        (hidden_grad * factor[1]).astype(BF16),
-        gated_hidden[...],
-    ]
+    grads[0] = (hidden_grad * factor[0]).astype(BF16)
+    grads[1] = (hidden_grad * factor[1]).astype(BF16)
+    for copy in tok_sent + gate_sent + half_sent + sum_sent + res_sent:
+        copy.wait_send()
+
+
+def update_kernel(
+    student, grads, rows, resid, latent, slope,
+    student_ref, new_gu_ref, new_dn_ref, fresh, store_sem,
+):
+    n, tok_rows, width = rows.shape[1:]
+    stores = [pltpu.make_async_copy(student, student_ref, store_sem.at[3])]
+    stores[0].start()
     targets = [new_gu_ref.at[0, 0], new_gu_ref.at[0, 1], new_dn_ref.at[0]]
     tile = min(width, 256)
-    stores = []
-    for matrix in (2, 0, 1):
+    for matrix in range(3):
         source = resid if matrix == 2 else rows
         for side in range(2):
             for first in range(0, width, tile):
                 block = source[side, :, :, first : first + tile].reshape(n * tok_rows, tile)
                 grad = jnp.dot(grads[matrix], block, preferred_element_type=F32)
                 cols = slice(side * width + first, side * width + first + tile)
-                slope[matrix, :, cols] = latent[matrix, :, cols] - learn_rate * (
+                fresh[matrix, :, cols] = latent[matrix, :, cols] - learn_rate * (
                     slope[matrix, :, cols] * grad
                 )
-        store = pltpu.make_async_copy(slope.at[matrix], targets[matrix], store_sem.at[matrix])
+        store = pltpu.make_async_copy(fresh.at[matrix], targets[matrix], store_sem.at[matrix])
         store.start()
         stores.append(store)
     for store in stores:
@@ -366,34 +374,35 @@
     dma = pltpu.SemaphoreType.DMA
     block = (n, tok_rows, width)
     vmem = pl.BlockSpec(memory_space=pltpu.VMEM)
-    hbm = pl.BlockSpec(memory_space=pl.ANY)
-    return pl.pallas_call(
+    hbm = pl.BlockSpec(memory_space=pltpu.HBM)
+    inputs = (tokens, teacher, expert_ids.T, gate_codes.T, gate_up_latent, down_latent)
+    state = pl.pallas_call(
         functools.partial(dense_kernel, n_inner, n_outer),
         out_shape=(
             jax.ShapeDtypeStruct(tokens.shape, BF16),
-            jax.ShapeDtypeStruct(gate_up_latent.shape, F32),
-            jax.ShapeDtypeStruct(down_latent.shape, F32),
+            jax.ShapeDtypeStruct((3, hid, n * tok_rows), BF16),
+            jax.ShapeDtypeStruct((2, *block), BF16),
+            jax.ShapeDtypeStruct((2, *block), BF16),
+            jax.ShapeDtypeStruct((3, hid, full), F32),
+            jax.ShapeDtypeStruct((3, hid, full), F32),
         ),
-        in_specs=[vmem, vmem, vmem, vmem, hbm, hbm],
-        out_specs=(vmem, hbm, hbm),
+        in_specs=[hbm] * 6,
+        out_specs=(vmem,) * 6,
         scratch_shapes=[
-            pltpu.VMEM((2, *block), BF16),
-            pltpu.VMEM((2, *block), BF16),
+            pltpu.VMEM((tok_rows, width), BF16),
+            pltpu.VMEM(expert_ids.shape[::-1], jnp.int32),
+            pltpu.VMEM(expert_ids.shape[::-1], jnp.int32),
             pltpu.VMEM((tok_rows, width), BF16),
             pltpu.VMEM((sublanes, LANES), F32),
             pltpu.VMEM((n, sublanes, LANES), F32),
-            pltpu.VMEM((3, hid, full), F32),
             pltpu.VMEM((3, hid, full), BF16),
-            pltpu.VMEM((3, hid, full), F32),
-            pltpu.VMEM((hid, n * tok_rows), BF16),
             pltpu.VMEM((2, hid, n * tok_rows), F32),
             pltpu.VMEM(block, BF16),
             pltpu.VMEM(block, BF16),
             pltpu.VMEM(block, F32),
             pltpu.VMEM(block, BF16),
             pltpu.VMEM(block, BF16),
-            dma((3,)),
-            dma((3,)),
+            dma((7,)),
             dma((n,)),
             dma((n,)),
             dma((gather_sends,)),
@@ -408,9 +417,21 @@
             dma((n,)),
         ],
         compiler_params=pltpu.CompilerParams(
-            collective_id=0, has_side_effects=True, vmem_limit_bytes=40 * 1024 * 1024
+            collective_id=0, has_side_effects=True, vmem_limit_bytes=24 * 1024 * 1024
         ),
-    )(tokens, teacher, expert_ids, gate_codes, gate_up_latent, down_latent)
+    )(*[pltpu.with_memory_space_constraint(value, pltpu.HBM) for value in inputs])
+    return pl.pallas_call(
+        update_kernel,
+        out_shape=(
+            jax.ShapeDtypeStruct(tokens.shape, BF16),
+            jax.ShapeDtypeStruct(gate_up_latent.shape, F32),
+            jax.ShapeDtypeStruct(down_latent.shape, F32),
+        ),
+        in_specs=[vmem] * 6,
+        out_specs=(hbm,) * 3,
+        scratch_shapes=[pltpu.VMEM((3, hid, full), F32), dma((4,))],
+        compiler_params=pltpu.CompilerParams(vmem_limit_bytes=24 * 1024 * 1024),
+    )(*state)
 
 
 def on_device(tokens, teacher, expert_ids, gate_codes, gate_up_latent, down_latent):

time: 44.1 us -> 35.9 us (0.81)
  local copies, waits for them, and re-layouts: 8.22 us -> 0 us
    unnamed x13 -> x0, local copies, waits for them, and re-layouts: 8.22 us -> none
    pallas_call x1, Pallas kernels: 34.8 us -> 33 us  [dense_step(): pl.pallas_call(functools.partial(dense_kernel, n_inner, n_outer), out_sha...]
    pallas_call x0 -> x1, Pallas kernels: none -> 1.72 us  [dense_step(): pl.pallas_call(update_kernel, out_shape=(jax.ShapeDtypeStruct(tokens.shap...]
where the time goes in v2:
time: 35.9 us; the launch traced here: 35.4 us
  Pallas kernels  34.7 us (97%)
  between operations  0.64 us (2%)
    pallas_call x1, Pallas kernels, dense_step(): pl.pallas_call(functools.partial(dense_kernel, n_inner, n_outer), out_sha...  33 us
    pallas_call x1, Pallas kernels, dense_step(): pl.pallas_call(update_kernel, out_shape=(jax.ShapeDtypeStruct(tokens.shap...  1.72 us

profile of v2, /device:TPU:0, one launch (start us, length us, event | category | flops | bytes accessed | tf_op | source)
XLA Modules:
  0.0 35.4 jit_solution(6012423418762418889)
XLA Ops:
  0.6 33.0 %shard_map.85 = (bf16[32,512]{1,0:T(8,128)(2,1)S(1)}, bf16[3,192,256]{2,1,0:T(8,128)(2,1)S(1)}, bf16[2,8,32,512]{3,2,1,0:T(8,128)(2,1)S(1)}, bf16[2,8,32,512]{3,...) custom-call(bf16[32,512]{1,0:T(8,128)(2,1)} %tokens_ref.1, ...), custom_call_target="tpu_custom_call" | custom-call | tf_op jit(solution)/shard_map/pallas_call | solution.py:379
  33.6 1.7 %shard_map.86 = (bf16[32,512]{1,0:T(8,128)(2,1)}, f32[1,2,192,1024]{3,2,1,0:T(8,128)}, f32[1,192,1024]{2,1,0:T(8,128)}) custom-call(bf16[32,512]{1,0:T(8,128)(2,1)S(1)} %get-tuple-element.9.student, bf16[3,192,256]{2,1,0:T(8,128)(2,1)S(1)} %get-tuple-element.10.grads, bf16[2,8,32,512]{3,2,1,0:T(8,128)(2,1)S(1)} %get-tuple-element.11.rows, ...), custom_call_target="tpu_custom_call" | custom-call | tf_op jit(solution)/shard_map/pallas_call | solution.py:423

commit v3 on v2

--- a/solution.py
+++ b/solution.py
@@ -116,9 +116,9 @@
     tokens_ref, teacher_ref, ids_ref, codes_ref, gu_ref, dn_ref,
     student, grads, rows, resid, latent, slope,
     teacher, ids, codes, resid_own, gates_own, gates, weight,
-    factor, half_out, half_in, mine, sums, returned,
+    factor, half_out, half_in, mine, sums, crossed, returned,
     load_sem, gate_send, gate_recv, tok_send, tok_recv, tok_rep,
-    half_send, half_recv, sum_send, sum_recv, res_send, res_recv, res_rep,
+    half_send, half_recv, sum_send, sum_recv, cross_recv, res_send, res_recv, res_rep,
 ):
     n = n_inner * n_outer
     tok_rows, width = tokens_ref.shape
@@ -227,9 +227,9 @@
             part = pl.ds(pl.multiple_of(at * piece, piece), piece)
             value = latent[matrix, part, :]
             row_scale = jnp.mean(jnp.abs(value), axis=-1, keepdims=True) + 1e-06
-            normed = value / row_scale
-            lower = jnp.tanh(4.0 * (normed - 0.5))
-            upper = jnp.tanh(4.0 * (normed + 0.5))
+            steep = value * (4.0 / row_scale)
+            lower = jnp.tanh(steep - 2.0)
+            upper = jnp.tanh(steep + 2.0)
             weight[matrix, part, :] = (row_scale * (0.5 * root) * (lower + upper)).astype(BF16)
             slope[matrix, part, :] = (2.0 * root) * (2.0 - lower * lower - upper * upper)
             return carry
@@ -288,26 +288,55 @@
         jnp.dot(hidden_t, weight[2, :, other_cols], preferred_element_type=F32)
         .astype(BF16).reshape(n, tok_rows, width)
     )
-    order = [peer_at(step) for step in range(1, n)] + [(me, None)]
+    inner_order = [inner_at(step) for step in range(1, n_inner)] + [inner]
     half_sent = []
-    for slot, _ in order:
-        copy = remote(half_out.at[slot], half_in.at[slot], half_send.at[slot], half_recv.at[slot], partner)
-        copy.start()
-        half_sent.append(copy)
+
+    def half_copy(slot):
+        return remote(
+            half_out.at[slot], half_in.at[slot], half_send.at[slot], half_recv.at[slot], partner
+        )
+
+    for across in range(1, n_outer + 1):
+        for at in inner_order:
+            copy = half_copy(at * n_outer + outer_at(across))
+            copy.start()
+            half_sent.append(copy)
     mine[...] = jnp.dot(
         hidden_t, weight[2, :, own_cols], preferred_element_type=F32
     ).reshape(n, tok_rows, width)
 
     sum_sent = []
-    for at, (slot, device) in enumerate(order):
-        half_sent[at].wait_recv()
+    for across in range(1, n_outer):
+        for at in inner_order:
+            slot = at * n_outer + outer_at(across)
+            half_copy(slot).wait_recv()
+            sums[slot] = (mine[slot] + half_in[slot].astype(F32)).astype(BF16)
+            landing = at * n_outer + outer
+            copy = remote(
+                sums.at[slot], crossed.at[landing], sum_send.at[slot], cross_recv.at[landing],
+                {"outer": outer_at(across)},
+            )
+            copy.start()
+            sum_sent.append(copy)
+
+    mixed = None
+    for at in inner_order:
+        slot = at * n_outer + outer
+        half_copy(slot).wait_recv()
         total = mine[slot] + half_in[slot].astype(F32)
-        if device is None:
-            mine[slot] = total
+        for across in range(1, n_outer):
+            landing = at * n_outer + outer_at(-across)
+            remote(
+                sums.at[slot], crossed.at[landing], sum_send.at[0], cross_recv.at[landing], partner
+            ).wait_recv()
+            total = total + crossed[landing].astype(F32)
+        if at is inner:
+            mixed = total
         else:
             sums[slot] = total.astype(BF16)
             copy = remote(
-                sums.at[slot], returned.at[me], sum_send.at[at], sum_recv.at[me], device
+                sums.at[slot], returned.at[inner], sum_send.at[slot], sum_recv.at[inner],
+                {"inner": at},
             )
             copy.start()
             sum_sent.append(copy)
@@ -315,9 +344,8 @@
     factor[0] = gate_row * pre_up * sigmoid_gate * (1.0 + pre_gate * (1.0 - sigmoid_gate))
     factor[1] = gate_row * activated
 
-    mixed = mine[me]
-    for step in range(1, n):
-        slot = peer_at(-step)[0]
+    for step in range(1, n_inner):
+        slot = inner_at(-step)
         remote(resid_own, returned.at[slot], sum_send.at[0], sum_recv.at[slot], partner).wait_recv()
         mixed = mixed + returned[slot].astype(F32)
     student[...] = mixed.astype(BF16)
@@ -402,10 +430,12 @@
             pltpu.VMEM(block, F32),
             pltpu.VMEM(block, BF16),
             pltpu.VMEM(block, BF16),
+            pltpu.VMEM((n_inner, tok_rows, width), BF16),
             dma((7,)),
             dma((n,)),
             dma((n,)),
             dma((gather_sends,)),
+            dma((n,)),
             dma((n,)),
             dma((n,)),
             dma((n,)),

time: 35.9 us -> 36.4 us (1.014)
  Pallas kernels: 34.7 us -> 35.1 us
    pallas_call x1, Pallas kernels: 33 us -> 33.4 us  [dense_step(): pl.pallas_call(functools.partial(dense_kernel, n_inner, n_outer), out_sha...]
where the time goes in v3:
time: 36.4 us; the launch traced here: 35.8 us
  Pallas kernels  35.1 us (96%)
  between operations  0.64 us (2%)
    pallas_call x1, Pallas kernels, dense_step(): pl.pallas_call(functools.partial(dense_kernel, n_inner, n_outer), out_sha...  33.4 us
    pallas_call x1, Pallas kernels, dense_step(): pl.pallas_call(update_kernel, out_shape=(jax.ShapeDtypeStruct(tokens.shap...  1.72 us

profile of v3, /device:TPU:0, one launch (start us, length us, event | category | flops | bytes accessed | tf_op | source)
XLA Modules:
  0.0 35.8 jit_solution(15384217352361942307)
XLA Ops:
  0.6 33.4 %shard_map.85 = (bf16[32,512]{1,0:T(8,128)(2,1)S(1)}, bf16[3,192,256]{2,1,0:T(8,128)(2,1)S(1)}, bf16[2,8,32,512]{3,2,1,0:T(8,128)(2,1)S(1)}, bf16[2,8,32,512]{3,...) custom-call(bf16[32,512]{1,0:T(8,128)(2,1)} %tokens_ref.1, ...), custom_call_target="tpu_custom_call" | custom-call | tf_op jit(solution)/shard_map/pallas_call | solution.py:407
  34.1 1.7 %shard_map.86 = (bf16[32,512]{1,0:T(8,128)(2,1)}, f32[1,2,192,1024]{3,2,1,0:T(8,128)}, f32[1,192,1024]{2,1,0:T(8,128)}) custom-call(bf16[32,512]{1,0:T(8,128)(2,1)S(1)} %get-tuple-element.9.student, bf16[3,192,256]{2,1,0:T(8,128)(2,1)S(1)} %get-tuple-element.10.grads, bf16[2,8,32,512]{3,2,1,0:T(8,128)(2,1)S(1)} %get-tuple-element.11.rows, ...), custom_call_target="tpu_custom_call" | custom-call | tf_op jit(solution)/shard_map/pallas_call | solution.py:453

commit v4 on v2

--- a/solution.py
+++ b/solution.py
@@ -169,10 +169,8 @@
             copy.start()
             sent.append(copy)
 
-        for step in range(1, n_inner):
-            push(own, me, recv.at[me], {"inner": inner_at(step)})
-        for step in range(1, n_outer):
-            push(own, me, recv.at[me], {"outer": outer_at(step)})
+        for step in range(1, n):
+            push(own, me, recv.at[me], peer_at(step)[1])
         push(own, me, rep_recv.at[me], partner)
         return sent, push
 
@@ -180,18 +178,10 @@
         def arrived(slot):
             remote(own, buf.at[rep, slot], send.at[0], recv.at[slot], partner).wait_recv()
 
-        for step in range(1, n_inner):
-            slot = inner_at(-step) * n_outer + outer
+        for step in range(1, n):
+            slot = peer_at(-step)[0]
             arrived(slot)
-            for across in range(1, n_outer):
-                push(buf.at[rep, slot], slot, recv.at[slot], {"outer": outer_at(across)})
             push(buf.at[rep, slot], slot, rep_recv.at[slot], partner)
-            between()
-        for step in range(n_inner):
-            for across in range(1, n_outer):
-                slot = inner_at(-step) * n_outer + outer_at(-across)
-                arrived(slot)
-                push(buf.at[rep, slot], slot, rep_recv.at[slot], partner)
             between()
         for slot in range(n):
             remote(own, buf.at[1 - rep, slot], send.at[0], rep_recv.at[slot], partner).wait_recv()
@@ -370,7 +360,7 @@
     tok_rows, width = tokens.shape
     hid, full = down_latent.shape[1:]
     sublanes = -(-n // 8) * 8
-    gather_sends = (n_inner - 1) * (1 + n_outer) + (n_outer - 1) * (1 + n_inner) + 1
+    gather_sends = 2 * n - 1
     dma = pltpu.SemaphoreType.DMA
     block = (n, tok_rows, width)
     vmem = pl.BlockSpec(memory_space=pltpu.VMEM)

time: 35.9 us -> 35.2 us (0.981)
  Pallas kernels: 34.7 us -> 34 us
    pallas_call x1, Pallas kernels: 33 us -> 32.3 us  [dense_step(): pl.pallas_call(functools.partial(dense_kernel, n_inner, n_outer), out_sha...]
where the time goes in v4:
time: 35.2 us; the launch traced here: 34.6 us
  Pallas kernels  34 us (97%)
  between operations  0.64 us (2%)
    pallas_call x1, Pallas kernels, dense_step(): pl.pallas_call(functools.partial(dense_kernel, n_inner, n_outer), out_sha...  32.3 us
    pallas_call x1, Pallas kernels, dense_step(): pl.pallas_call(update_kernel, out_shape=(jax.ShapeDtypeStruct(tokens.shap...  1.71 us

profile of v4, /device:TPU:0, one launch (start us, length us, event | category | flops | bytes accessed | tf_op | source)
XLA Modules:
  0.0 34.6 jit_solution(7873344223027056875)
XLA Ops:
  0.6 32.3 %shard_map.85 = (bf16[32,512]{1,0:T(8,128)(2,1)S(1)}, bf16[3,192,256]{2,1,0:T(8,128)(2,1)S(1)}, bf16[2,8,32,512]{3,2,1,0:T(8,128)(2,1)S(1)}, bf16[2,8,32,512]{3,...) custom-call(bf16[32,512]{1,0:T(8,128)(2,1)} %tokens_ref.1, ...), custom_call_target="tpu_custom_call" | custom-call | tf_op jit(solution)/shard_map/pallas_call | solution.py:369
  32.9 1.7 %shard_map.86 = (bf16[32,512]{1,0:T(8,128)(2,1)}, f32[1,2,192,1024]{3,2,1,0:T(8,128)}, f32[1,192,1024]{2,1,0:T(8,128)}) custom-call(bf16[32,512]{1,0:T(8,128)(2,1)S(1)} %get-tuple-element.9.student, bf16[3,192,256]{2,1,0:T(8,128)(2,1)S(1)} %get-tuple-element.10.grads, bf16[2,8,32,512]{3,2,1,0:T(8,128)(2,1)S(1)} %get-tuple-element.11.rows, ...), custom_call_target="tpu_custom_call" | custom-call | tf_op jit(solution)/shard_map/pallas_call | solution.py:413

commit v5 on v0

--- a/solution.py
+++ b/solution.py
@@ -1,8 +1,11 @@
+import functools
 import math
 
 import jax
 import jax.numpy as jnp
 from jax import lax
+from jax.experimental import pallas as pl
+from jax.experimental.pallas import tpu as pltpu
 from jax.sharding import PartitionSpec as P
 
 D = 1024
@@ -35,7 +38,7 @@
     return lax.all_to_all(outbox, ("inner", "outer"), split_axis=0, concat_axis=0, tiled=True)
 
 
-def on_device(tokens, teacher, expert_ids, gate_codes, gate_up_latent, down_latent):
+def routed_step(tokens, teacher, expert_ids, gate_codes, gate_up_latent, down_latent):
     experts = lax.axis_size("inner") * lax.axis_size("outer")
     tok_rows, top_count = expert_ids.shape
     part_width = tokens.shape[1]
@@ -98,6 +101,381 @@
     return (student_out, new_gate_up, new_down)
 
 
+MESH = pl.DeviceIdType.MESH
+LANES = 128
+BF16 = jnp.bfloat16
+F32 = jnp.float32
+
+
+def dot_t(a, b):
+    return lax.dot_general(a, b, (((1,), (1,)), ((), ())), preferred_element_type=F32)
+
+
+def dense_kernel(
+    n_inner, n_outer,
+    tokens_ref, teacher_ref, ids_ref, codes_ref, gu_ref, dn_ref,
+    student, grads, rows, resid, latent, slope,
+    teacher, ids, codes, resid_own, gates_own, gates, weight, factor, sums, returned,
+    load_sem, gate_send, gate_recv, tok_send, tok_recv, pair_send, pair_recv,
+    sum_send, sum_recv, res_send, res_recv, res_rep,
+):
+    n = n_inner * n_outer
+    tok_rows, width = tokens_ref.shape
+    part = tok_rows // 2
+    count = n * part
+    hid = latent.shape[1]
+    inner, outer, rep = lax.axis_index("inner"), lax.axis_index("outer"), lax.axis_index("rep")
+    me = inner * n_outer + outer
+    sides = (rep, 1 - rep)
+    partner = {"rep": 1 - rep}
+
+    def peer_at(step):
+        peer = lax.rem(me + step + n, n)
+        return peer, {"inner": peer // n_outer, "outer": lax.rem(peer, n_outer)}
+
+    def remote(source, target, send, recv, device):
+        return pltpu.make_async_remote_copy(
+            src_ref=source, dst_ref=target, send_sem=send, recv_sem=recv,
+            device_id=device, device_id_type=MESH,
+        )
+
+    others = [(step, side) for step in range(n) for side in range(2) if step or side]
+
+    def part_rows(side):
+        return pl.ds(pl.multiple_of(side * part, part), part)
+
+    loads = [
+        pltpu.make_async_copy(gu_ref.at[0, 0], latent.at[0], load_sem.at[0]),
+        pltpu.make_async_copy(gu_ref.at[0, 1], latent.at[1], load_sem.at[1]),
+        pltpu.make_async_copy(dn_ref.at[0], latent.at[2], load_sem.at[2]),
+        pltpu.make_async_copy(
+            tokens_ref.at[part_rows(rep)], rows.at[rep, rep, me], load_sem.at[3]
+        ),
+        pltpu.make_async_copy(teacher_ref, teacher, load_sem.at[4]),
+        pltpu.make_async_copy(ids_ref, ids, load_sem.at[5]),
+        pltpu.make_async_copy(codes_ref, codes, load_sem.at[6]),
+    ]
+    for load in loads:
+        load.start()
+
+    barrier = pltpu.get_barrier_semaphore()
+    for step, side in others:
+        device = dict(peer_at(step)[1], rep=sides[side])
+        pl.semaphore_signal(barrier, inc=1, device_id=device, device_id_type=MESH)
+    pl.semaphore_wait(barrier, len(others))
+
+    sent = []
+
+    def spread(source_of, target_of, send, recv, slot_of):
+        for at, (step, side) in enumerate(others):
+            peer, device = peer_at(step)
+            copy = remote(
+                source_of(peer, sides[side]), target_of(sides[side]),
+                send.at[at], recv.at[slot_of], dict(device, rep=sides[side]),
+            )
+            copy.start()
+            sent.append(copy)
+
+    def arrived(source, target_of, send, recv, step, side):
+        peer = peer_at(-step)[0]
+        slot = sides[side] * n + peer
+        remote(
+            source, target_of(sides[side], peer), send.at[0], recv.at[slot], partner
+        ).wait_recv()
+
+    mine = rep * n + me
+    spread(
+        lambda peer, side: tokens_ref.at[part_rows(side)],
+        lambda side: rows.at[side, rep, me],
+        tok_send, tok_recv, mine,
+    )
+
+    loads[5].wait()
+    loads[6].wait()
+    gate_of = codes[...].astype(F32) * (1.0 / 65536.0)
+    line = lax.broadcasted_iota(jnp.int32, (gates_own.shape[1], tok_rows), 0)
+    table = jnp.zeros((gates_own.shape[1], tok_rows), F32)
+    for expert in range(n):
+        row = jnp.sum(jnp.where(ids[...] == expert, gate_of, 0.0), axis=0, keepdims=True)
+        table = jnp.where(line == expert, row, table)
+    gates_own[...] = jnp.zeros_like(gates_own)
+    for half in range(2):
+        gates_own[half, :, :part] = table[:, half * part : (half + 1) * part]
+    for step in range(1, n):
+        copy = remote(
+            gates_own, gates.at[me], gate_send.at[step - 1], gate_recv.at[me], peer_at(step)[1]
+        )
+        copy.start()
+        sent.append(copy)
+    gates[me] = gates_own[...]
+
+    fan_root = [1.0 / math.sqrt(latent.shape[2])] * 2 + [1.0 / math.sqrt(2 * hid)]
+    piece = 32
+
+    def soften_rows(matrix):
+        root = fan_root[matrix]
+
+        def body(at, carry):
+            lines = pl.ds(pl.multiple_of(at * piece, piece), piece)
+            value = latent[matrix, lines, :]
+            row_scale = jnp.mean(jnp.abs(value), axis=-1, keepdims=True) + 1e-06
+            steep = value * (4.0 / row_scale)
+            lower = jnp.tanh(steep - 2.0)
+            upper = jnp.tanh(steep + 2.0)
+            weight[rep, matrix, lines, :] = (row_scale * (0.5 * root) * (lower + upper)).astype(BF16)
+            slope[matrix, lines, :] = (2.0 * root) * (2.0 - lower * lower - upper * upper)
+            return carry
+
+        lax.fori_loop(0, hid // piece, body, 0)
+
+    weight_copies = []
+    for matrix in range(3):
+        loads[matrix].wait()
+        soften_rows(matrix)
+        copy = remote(
+            weight.at[rep, matrix], weight.at[rep, matrix],
+            pair_send.at[matrix], pair_recv.at[matrix], partner,
+        )
+        copy.start()
+        weight_copies.append(copy)
+    sent.extend(weight_copies)
+
+    for step in range(1, n):
+        slot = peer_at(-step)[0]
+        remote(gates_own, gates.at[slot], gate_send.at[0], gate_recv.at[slot], partner).wait_recv()
+    per_row = LANES // part
+
+    def gates_for(half):
+        return jnp.concatenate(
+            [
+                sum(
+                    pltpu.roll(gates[base + at, half, pl.ds(me, 1), :], at * part, 1) if at
+                    else gates[base, half, pl.ds(me, 1), :]
+                    for at in range(per_row)
+                )
+                for base in range(0, n, per_row)
+            ],
+            axis=1,
+        )
+
+    both_gates = [gates_for(half) for half in range(2)]
+    own_gate = jnp.where(rep == 0, both_gates[0], both_gates[1])
+    other_gate = jnp.where(rep == 0, both_gates[1], both_gates[0])
+
+    def features(buf, half, column):
+        return buf[half, column].reshape(count, width)
+
+    def forward(units, half, gate_row):
+        both = weight[units, 0:2].reshape(2 * hid, 2 * width)
+        pre = dot_t(both[:, :width], features(rows, half, 0))
+        pre = pre + dot_t(both[:, width:], features(rows, half, 1))
+        pre_gate, pre_up = pre[:hid], pre[hid:]
+        sigmoid_gate = jax.nn.sigmoid(pre_gate)
+        activated = pre_gate * sigmoid_gate
+        return pre_gate, pre_up, sigmoid_gate, activated, activated * pre_up * gate_row
+
+    def keep(half, gate_row, values):
+        pre_gate, pre_up, sigmoid_gate, activated, hidden = values
+        cols = pl.ds(pl.multiple_of(half * count, count), count)
+        grads[2, :, cols] = hidden.astype(BF16)
+        factor[0, half] = gate_row * pre_up * sigmoid_gate * (1.0 + pre_gate * (1.0 - sigmoid_gate))
+        factor[1, half] = gate_row * activated
+
+    loads[3].wait()
+    for step, side in others:
+        arrived(
+            tokens_ref.at[part_rows(0)], lambda side, peer: rows.at[rep, side, peer],
+            tok_send, tok_recv, step, side,
+        )
+    rows_copy = remote(rows.at[rep], rows.at[rep], pair_send.at[3], pair_recv.at[3], partner)
+    rows_copy.start()
+    sent.append(rows_copy)
+    own_values = forward(rep, rep, own_gate)
+    out = jnp.dot(own_values[-1].T.astype(BF16), weight[rep, 2], preferred_element_type=F32)
+    for copy in weight_copies:
+        copy.wait_recv()
+    hidden = forward(1 - rep, rep, own_gate)[-1]
+    out = out + jnp.dot(hidden.T.astype(BF16), weight[1 - rep, 2], preferred_element_type=F32)
+    for column in range(2):
+        sums[column] = (
+            out[:, column * width : (column + 1) * width].astype(BF16).reshape(n, part, width)
+        )
+    spread(
+        lambda peer, side: sums.at[side, peer],
+        lambda side: returned.at[rep, me],
+        sum_send, sum_recv, mine,
+    )
+    returned[rep, me] = sums[rep, me]
+
+    keep(rep, own_gate, own_values)
+    rows_copy.wait_recv()
+    keep(1 - rep, other_gate, forward(rep, 1 - rep, other_gate))
+
+    loads[4].wait()
+    for step, side in others:
+        arrived(
+            resid_own.at[0], lambda side, peer: returned.at[side, peer],
+            sum_send, sum_recv, step, side,
+        )
+    for half in range(2):
+        mixed = returned[half, 0].astype(F32)
+        for peer in range(1, n):
+            mixed = mixed + returned[half, peer].astype(F32)
+        lines = slice(half * part, (half + 1) * part)
+        student[lines] = mixed.astype(BF16)
+        resid_own[half] = (mixed - teacher[lines].astype(F32)).astype(BF16)
+    spread(
+        lambda peer, side: resid_own.at[side],
+        lambda side: resid.at[side, rep, me],
+        res_send, res_recv, mine,
+    )
+    resid[rep, rep, me] = resid_own[rep]
+
+    def pass_on(column, peer, at):
+        copy = remote(
+            resid.at[rep, column, peer], resid.at[rep, column, peer],
+            res_send.at[2 * n + at], res_rep.at[column * n + peer], partner,
+        )
+        copy.start()
+        sent.append(copy)
+
+    pass_on(rep, me, 2 * n - 1)
+    for at, (step, side) in enumerate(others):
+        arrived(
+            resid_own.at[0], lambda side, peer: resid.at[rep, side, peer],
+            res_send, res_recv, step, side,
+        )
+        pass_on(sides[side], peer_at(-step)[0], at)
+
+    def backward(half):
+        down = weight[rep, 2]
+        hidden_grad = dot_t(down[:, :width], features(resid, half, 0))
+        hidden_grad = hidden_grad + dot_t(down[:, width:], features(resid, half, 1))
+        cols = pl.ds(pl.multiple_of(half * count, count), count)
+        grads[0, :, cols] = (hidden_grad * factor[0, half]).astype(BF16)
+        grads[1, :, cols] = (hidden_grad * factor[1, half]).astype(BF16)
+
+    backward(rep)
+    for column in range(2):
+        for peer in range(n):
+            remote(
+                resid_own.at[0], resid.at[1 - rep, column, peer],
+                res_send.at[0], res_rep.at[column * n + peer], partner,
+            ).wait_recv()
+    backward(1 - rep)
+    for copy in sent:
+        copy.wait_send()
+
+
+def update_kernel(
+    student, grads, rows, resid, latent, slope,
+    student_ref, new_gu_ref, new_dn_ref, fresh, store_sem,
+):
+    n, part, width = rows.shape[2:]
+    stores = [pltpu.make_async_copy(student, student_ref, store_sem.at[3])]
+    stores[0].start()
+    targets = [new_gu_ref.at[0, 0], new_gu_ref.at[0, 1], new_dn_ref.at[0]]
+    tile = min(width, 256)
+    for matrix in range(3):
+        source = resid if matrix == 2 else rows
+        for side in range(2):
+            for first in range(0, width, tile):
+                block = source[:, side, :, :, first : first + tile].reshape(2 * n * part, tile)
+                grad = jnp.dot(grads[matrix], block, preferred_element_type=F32)
+                cols = slice(side * width + first, side * width + first + tile)
+                fresh[matrix, :, cols] = latent[matrix, :, cols] - learn_rate * (
+                    slope[matrix, :, cols] * grad
+                )
+        store = pltpu.make_async_copy(fresh.at[matrix], targets[matrix], store_sem.at[matrix])
+        store.start()
+        stores.append(store)
+    for store in stores:
+        store.wait()
+
+
+def dense_step(tokens, teacher, expert_ids, gate_codes, gate_up_latent, down_latent):
+    n_inner, n_outer = lax.axis_size("inner"), lax.axis_size("outer")
+    n = n_inner * n_outer
+    tok_rows, width = tokens.shape
+    hid, full = down_latent.shape[1:]
+    sublanes = -(-n // 8) * 8
+    part = tok_rows // 2
+    dma = pltpu.SemaphoreType.DMA
+    halves = (2, n, part, width)
+    vmem = pl.BlockSpec(memory_space=pltpu.VMEM)
+    hbm = pl.BlockSpec(memory_space=pltpu.HBM)
+    inputs = (tokens, teacher, expert_ids.T, gate_codes.T, gate_up_latent, down_latent)
+    state = pl.pallas_call(
+        functools.partial(dense_kernel, n_inner, n_outer),
+        out_shape=(
+            jax.ShapeDtypeStruct(tokens.shape, BF16),
+            jax.ShapeDtypeStruct((3, hid, n * tok_rows), BF16),
+            jax.ShapeDtypeStruct((2, *halves), BF16),
+            jax.ShapeDtypeStruct((2, *halves), BF16),
+            jax.ShapeDtypeStruct((3, hid, full), F32),
+            jax.ShapeDtypeStruct((3, hid, full), F32),
+        ),
+        in_specs=[hbm] * 6,
+        out_specs=(vmem,) * 6,
+        scratch_shapes=[
+            pltpu.VMEM((tok_rows, width), BF16),
+            pltpu.VMEM(expert_ids.shape[::-1], jnp.int32),
+            pltpu.VMEM(expert_ids.shape[::-1], jnp.int32),
+            pltpu.VMEM((2, part, width), BF16),
+            pltpu.VMEM((2, sublanes, LANES), F32),
+            pltpu.VMEM((n, 2, sublanes, LANES), F32),
+            pltpu.VMEM((2, 3, hid, full), BF16),
+            pltpu.VMEM((2, 2, hid, n * part), F32),
+            pltpu.VMEM(halves, BF16),
+            pltpu.VMEM(halves, BF16),
+            dma((7,)),
+            dma((n,)),
+            dma((n,)),
+            dma((2 * n,)),
+            dma((2 * n,)),
+            dma((4,)),
+            dma((4,)),
+            dma((2 * n,)),
+            dma((2 * n,)),
+            dma((4 * n,)),
+            dma((2 * n,)),
+            dma((2 * n,)),
+        ],
+        compiler_params=pltpu.CompilerParams(
+            collective_id=0, has_side_effects=True, vmem_limit_bytes=24 * 1024 * 1024
+        ),
+    )(*[pltpu.with_memory_space_constraint(value, pltpu.HBM) for value in inputs])
+    return pl.pallas_call(
+        update_kernel,
+        out_shape=(
+            jax.ShapeDtypeStruct(tokens.shape, BF16),
+            jax.ShapeDtypeStruct(gate_up_latent.shape, F32),
+            jax.ShapeDtypeStruct(down_latent.shape, F32),
+        ),
+        in_specs=[vmem] * 6,
+        out_specs=(hbm,) * 3,
+        scratch_shapes=[pltpu.VMEM((3, hid, full), F32), dma((4,))],
+        compiler_params=pltpu.CompilerParams(vmem_limit_bytes=24 * 1024 * 1024),
+    )(*state)
+
+
+def on_device(tokens, teacher, expert_ids, gate_codes, gate_up_latent, down_latent):
+    experts = lax.axis_size("inner") * lax.axis_size("outer")
+    tok_rows, top_count = expert_ids.shape
+    whole_block = 2 * top_count >= experts
+    fits = (
+        lax.axis_size("rep") == 2
+        and LANES % tok_rows == 0
+        and tok_rows % 32 == 0
+        and experts <= LANES
+        and experts * tok_rows % (2 * LANES) == 0
+        and tokens.shape[1] % LANES == 0
+        and down_latent.shape[1] % 64 == 0
+    )
+    step = dense_step if whole_block and fits else routed_step
+    return step(tokens, teacher, expert_ids, gate_codes, gate_up_latent, down_latent)
+
+
 def solution(mesh):
     return jax.shard_map(
         on_device,

time: 86.3 us -> 34.4 us (0.40)
  Pallas kernels: 0 us -> 33.6 us
  waiting for transfers between devices: 23.3 us -> 0 us
  blocking collectives: 16.7 us -> 0 us
  between operations: 14.2 us -> 0.64 us
  starting transfers between devices: 13.2 us -> 0 us
  matrix products: 7.07 us -> 0 us
  other arithmetic: 5.84 us -> 0 us
  local copies, waits for them, and re-layouts: 5.57 us -> 0 us
    pallas_call x0 -> x2, Pallas kernels: none -> 33.6 us  [the longest x1 31.9 us: dense_step(): pl.pallas_call(functools.partial(dense_kernel, n_inner, n_outer), out_sha...]
    all_to_all x2 -> x0, waiting for transfers between devices: 16.2 us -> none  [the longest x1 9.19 us: combine_rows(): lax.all_to_all(outbox, ('inner', 'outer'), split_axis=0, concat_axis=0, t...]
    all_to_all x2 -> x0, starting transfers between devices: 13.1 us -> none  [the longest x1 7.25 us: dispatch_rows(): lax.all_to_all(outbox, ('inner', 'outer'), split_axis=0, concat_axis=0, t...]
    all_to_all x1 -> x0, blocking collectives: 12.3 us -> none  [upstream_rows(): lax.all_to_all(outbox, ('inner', 'outer'), split_axis=0, concat_axis=0, t...]
    reduce_scatter x1 -> x0, waiting for transfers between devices: 7.15 us -> none  [on_device(): lax.psum_scatter(partial_out.astype(jnp.bfloat16), 'rep', scatter_dimensi...]
    dot_general x5 -> x0, matrix products: 7.07 us -> none  [the longest x1 2 us: on_device(): lax.dot_general(jnp.stack([gate_grad, up_grad]), expert_rows, (((2,), (0,...]
    all_gather x2 -> x0, blocking collectives: 4.34 us -> none  [the longest x1 2.17 us: on_device(): expert_rows = lax.all_gather(received, 'rep', axis=1, tiled=True)]
    reduce_sum x4 -> x0, other arithmetic: 2.17 us -> none  [the longest x2 1.86 us: soften(): row_scale = jnp.mean(jnp.abs(latent), axis=-1, keepdims=True) + 1e-06]
  transfers between devices with their start and end apart: 3 -> 0, of which waited for: 3 -> 0; matrix products, arithmetic and copies ran while one was open for 2% -> 0% of each run, Pallas kernels for 0% -> 0%
where the time goes in v5:
time: 34.4 us; the launch traced here: 34.2 us
  Pallas kernels  33.6 us (98%)
  between operations  0.64 us (2%)
    pallas_call x1, Pallas kernels, dense_step(): pl.pallas_call(functools.partial(dense_kernel, n_inner, n_outer), out_sha...  31.9 us
    pallas_call x1, Pallas kernels, dense_step(): pl.pallas_call(update_kernel, out_shape=(jax.ShapeDtypeStruct(tokens.shap...  1.72 us

profile of v5, /device:TPU:0, one launch (start us, length us, event | category | flops | bytes accessed | tf_op | source)
XLA Modules:
  0.0 34.2 jit_solution(4269555724215202736)
XLA Ops:
  0.6 31.9 %shard_map.85 = (bf16[32,512]{1,0:T(8,128)(2,1)S(1)}, bf16[3,192,256]{2,1,0:T(8,128)(2,1)S(1)}, bf16[2,2,8,16,512]{4,3,2,1,0:T(8,128)(2,1)S(1)}, bf16[2,2,8,16,5...) custom-call(bf16[32,512]{1,0:T(8,128)(2,1)} %tokens_ref.1, ...), custom_call_target="tpu_custom_call" | custom-call | tf_op jit(solution)/shard_map/pallas_call | solution.py:408
  32.5 1.7 %shard_map.86 = (bf16[32,512]{1,0:T(8,128)(2,1)}, f32[1,2,192,1024]{3,2,1,0:T(8,128)}, f32[1,192,1024]{2,1,0:T(8,128)}) custom-call(bf16[32,512]{1,0:T(8,128)(2,1)S(1)} %get-tuple-element.9.student, bf16[3,192,256]{2,1,0:T(8,128)(2,1)S(1)} %get-tuple-element.10.grads, bf16[2,2,8,16,512]{4,3,2,1,0:T(8,128)(2,1)S(1)} %get-tuple-element.11.rows, ...), custom_call_target="tpu_custom_call" | custom-call | tf_op jit(solution)/shard_map/pallas_call | solution.py:448

commit v6 on v5

--- a/solution.py
+++ b/solution.py
@@ -155,13 +155,12 @@
         pltpu.make_async_copy(ids_ref, ids, load_sem.at[5]),
         pltpu.make_async_copy(codes_ref, codes, load_sem.at[6]),
     ]
-    for load in loads:
-        load.start()
-
     barrier = pltpu.get_barrier_semaphore()
     for step, side in others:
         device = dict(peer_at(step)[1], rep=sides[side])
         pl.semaphore_signal(barrier, inc=1, device_id=device, device_id_type=MESH)
+    for load in loads:
+        load.start()
     pl.semaphore_wait(barrier, len(others))
 
     sent = []
@@ -226,7 +225,7 @@
             slope[matrix, lines, :] = (2.0 * root) * (2.0 - lower * lower - upper * upper)
             return carry
 
-        lax.fori_loop(0, hid // piece, body, 0)
+        lax.fori_loop(0, hid // piece, body, 0, unroll=3 if hid % (3 * piece) == 0 else 2)
 
     weight_copies = []
     for matrix in range(3):
@@ -287,14 +286,12 @@
             tokens_ref.at[part_rows(0)], lambda side, peer: rows.at[rep, side, peer],
             tok_send, tok_recv, step, side,
         )
-    rows_copy = remote(rows.at[rep], rows.at[rep], pair_send.at[3], pair_recv.at[3], partner)
-    rows_copy.start()
-    sent.append(rows_copy)
     own_values = forward(rep, rep, own_gate)
     out = jnp.dot(own_values[-1].T.astype(BF16), weight[rep, 2], preferred_element_type=F32)
-    for copy in weight_copies:
-        copy.wait_recv()
+    weight_copies[0].wait_recv()
+    weight_copies[1].wait_recv()
     hidden = forward(1 - rep, rep, own_gate)[-1]
+    weight_copies[2].wait_recv()
     out = out + jnp.dot(hidden.T.astype(BF16), weight[1 - rep, 2], preferred_element_type=F32)
     for column in range(2):
         sums[column] = (
@@ -305,6 +302,9 @@
         lambda side: returned.at[rep, me],
         sum_send, sum_recv, mine,
     )
+    rows_copy = remote(rows.at[rep], rows.at[rep], pair_send.at[3], pair_recv.at[3], partner)
+    rows_copy.start()
+    sent.append(rows_copy)
     returned[rep, me] = sums[rep, me]
 
     keep(rep, own_gate, own_values)

time: 34.4 us -> 34.4 us (level)
  no operation moved by 1% of the time
where the time goes in v6:
time: 34.4 us; the launch traced here: 34.2 us
  Pallas kernels  33.6 us (98%)
  between operations  0.64 us (2%)
    pallas_call x1, Pallas kernels, dense_step(): pl.pallas_call(functools.partial(dense_kernel, n_inner, n_outer), out_sha...  31.9 us
    pallas_call x1, Pallas kernels, dense_step(): pl.pallas_call(update_kernel, out_shape=(jax.ShapeDtypeStruct(tokens.shap...  1.71 us

profile of v6, /device:TPU:0, one launch (start us, length us, event | category | flops | bytes accessed | tf_op | source)
XLA Modules:
  0.0 34.2 jit_solution(16793548488726603063)
XLA Ops:
  0.6 31.9 %shard_map.85 = (bf16[32,512]{1,0:T(8,128)(2,1)S(1)}, bf16[3,192,256]{2,1,0:T(8,128)(2,1)S(1)}, bf16[2,2,8,16,512]{4,3,2,1,0:T(8,128)(2,1)S(1)}, bf16[2,2,8,16,5...) custom-call(bf16[32,512]{1,0:T(8,128)(2,1)} %tokens_ref.1, ...), custom_call_target="tpu_custom_call" | custom-call | tf_op jit(solution)/shard_map/pallas_call | solution.py:408
  32.5 1.7 %shard_map.86 = (bf16[32,512]{1,0:T(8,128)(2,1)}, f32[1,2,192,1024]{3,2,1,0:T(8,128)}, f32[1,192,1024]{2,1,0:T(8,128)}) custom-call(bf16[32,512]{1,0:T(8,128)(2,1)S(1)} %get-tuple-element.9.student, bf16[3,192,256]{2,1,0:T(8,128)(2,1)S(1)} %get-tuple-element.10.grads, bf16[2,2,8,16,512]{4,3,2,1,0:T(8,128)(2,1)S(1)} %get-tuple-element.11.rows, ...), custom_call_target="tpu_custom_call" | custom-call | tf_op jit(solution)/shard_map/pallas_call | solution.py:448

commit v7 on v6

--- a/solution.py
+++ b/solution.py
@@ -129,9 +129,10 @@
     sides = (rep, 1 - rep)
     partner = {"rep": 1 - rep}
 
-    def peer_at(step):
-        peer = lax.rem(me + step + n, n)
-        return peer, {"inner": peer // n_outer, "outer": lax.rem(peer, n_outer)}
+    def peer_at(step, sign=1):
+        at_inner = lax.rem(inner + sign * step[0] + n_inner, n_inner)
+        at_outer = lax.rem(outer + sign * step[1] + n_outer, n_outer)
+        return at_inner * n_outer + at_outer, {"inner": at_inner, "outer": at_outer}
 
     def remote(source, target, send, recv, device):
         return pltpu.make_async_remote_copy(
@@ -139,7 +140,11 @@
             device_id=device, device_id_type=MESH,
         )
 
-    others = [(step, side) for step in range(n) for side in range(2) if step or side]
+    steps = [(up, across) for up in range(n_inner) for across in range(n_outer)]
+    others = [(step, side) for step in steps for side in range(2) if any(step) or side]
+    lined = [((up, 0), 0) for up in range(1, n_inner)]
+    others = lined + [pair for pair in others if pair not in lined]
+    relayed = [(step, side) for step, side in others if all(step) and not side]
 
     def part_rows(side):
         return pl.ds(pl.multiple_of(side * part, part), part)
@@ -165,8 +170,10 @@
 
     sent = []
 
-    def spread(source_of, target_of, send, recv, slot_of):
+    def spread(source_of, target_of, send, recv, slot_of, skip=()):
         for at, (step, side) in enumerate(others):
+            if (step, side) in skip:
+                continue
             peer, device = peer_at(step)
             copy = remote(
                 source_of(peer, sides[side]), target_of(sides[side]),
@@ -176,17 +183,29 @@
             sent.append(copy)
 
     def arrived(source, target_of, send, recv, step, side):
-        peer = peer_at(-step)[0]
+        peer = peer_at(step, -1)[0]
         slot = sides[side] * n + peer
         remote(
             source, target_of(sides[side], peer), send.at[0], recv.at[slot], partner
         ).wait_recv()
 
+    def relay(source, buf, send, recv, step):
+        arrived(source, lambda side, peer: buf.at[rep, side, peer], send, recv, step, 0)
+        peer = peer_at(step, -1)[0]
+        for across in range(1, n_outer):
+            copy = remote(
+                buf.at[rep, rep, peer], buf.at[rep, rep, peer],
+                send.at[others.index(((step[0], across), 0))], recv.at[rep * n + peer],
+                {"outer": lax.rem(outer + across, n_outer)},
+            )
+            copy.start()
+            sent.append(copy)
+
     mine = rep * n + me
     spread(
         lambda peer, side: tokens_ref.at[part_rows(side)],
         lambda side: rows.at[side, rep, me],
-        tok_send, tok_recv, mine,
+        tok_send, tok_recv, mine, relayed,
     )
 
     loads[5].wait()
@@ -200,9 +219,9 @@
     gates_own[...] = jnp.zeros_like(gates_own)
     for half in range(2):
         gates_own[half, :, :part] = table[:, half * part : (half + 1) * part]
-    for step in range(1, n):
+    for at, step in enumerate(steps[1:]):
         copy = remote(
-            gates_own, gates.at[me], gate_send.at[step - 1], gate_recv.at[me], peer_at(step)[1]
+            gates_own, gates.at[me], gate_send.at[at], gate_recv.at[me], peer_at(step)[1]
         )
         copy.start()
         sent.append(copy)
@@ -237,10 +256,13 @@
         )
         copy.start()
         weight_copies.append(copy)
+        if matrix == 0:
+            for step, _ in lined:
+                relay(tokens_ref.at[part_rows(0)], rows, tok_send, tok_recv, step)
     sent.extend(weight_copies)
 
-    for step in range(1, n):
-        slot = peer_at(-step)[0]
+    for step in steps[1:]:
+        slot = peer_at(step, -1)[0]
         remote(gates_own, gates.at[slot], gate_send.at[0], gate_recv.at[slot], partner).wait_recv()
     per_row = LANES // part
 
@@ -281,7 +303,7 @@
         factor[1, half] = gate_row * activated
 
     loads[3].wait()
-    for step, side in others:
+    for step, side in others[len(lined):]:
         arrived(
             tokens_ref.at[part_rows(0)], lambda side, peer: rows.at[rep, side, peer],
             tok_send, tok_recv, step, side,
@@ -327,7 +349,7 @@
     spread(
         lambda peer, side: resid_own.at[side],
         lambda side: resid.at[side, rep, me],
-        res_send, res_recv, mine,
+        res_send, res_recv, mine, relayed,
     )
     resid[rep, rep, me] = resid_own[rep]
 
@@ -341,11 +363,14 @@
 
     pass_on(rep, me, 2 * n - 1)
     for at, (step, side) in enumerate(others):
-        arrived(
-            resid_own.at[0], lambda side, peer: resid.at[rep, side, peer],
-            res_send, res_recv, step, side,
-        )
-        pass_on(sides[side], peer_at(-step)[0], at)
+        if at < len(lined):
+            relay(resid_own.at[0], resid, res_send, res_recv, step)
+        else:
+            arrived(
+                resid_own.at[0], lambda side, peer: resid.at[rep, side, peer],
+                res_send, res_recv, step, side,
+            )
+        pass_on(sides[side], peer_at(step, -1)[0], at)
 
     def backward(half):
         down = weight[rep, 2]

time: 34.4 us -> 34.6 us (level)
  no operation moved by 1% of the time
where the time goes in v7:
time: 34.6 us; the launch traced here: 34.1 us
  Pallas kernels  33.5 us (97%)
  between operations  0.64 us (2%)
    pallas_call x1, Pallas kernels, dense_step(): pl.pallas_call(functools.partial(dense_kernel, n_inner, n_outer), out_sha...  31.8 us
    pallas_call x1, Pallas kernels, dense_step(): pl.pallas_call(update_kernel, out_shape=(jax.ShapeDtypeStruct(tokens.shap...  1.72 us

profile of v7, /device:TPU:0, one launch (start us, length us, event | category | flops | bytes accessed | tf_op | source)
XLA Modules:
  0.0 34.1 jit_solution(17309588292320208164)
XLA Ops:
  0.6 31.8 %shard_map.85 = (bf16[32,512]{1,0:T(8,128)(2,1)S(1)}, bf16[3,192,256]{2,1,0:T(8,128)(2,1)S(1)}, bf16[2,2,8,16,512]{4,3,2,1,0:T(8,128)(2,1)S(1)}, bf16[2,2,8,16,5...) custom-call(bf16[32,512]{1,0:T(8,128)(2,1)} %tokens_ref.1, ...), custom_call_target="tpu_custom_call" | custom-call | tf_op jit(solution)/shard_map/pallas_call | solution.py:433
  32.4 1.7 %shard_map.86 = (bf16[32,512]{1,0:T(8,128)(2,1)}, f32[1,2,192,1024]{3,2,1,0:T(8,128)}, f32[1,192,1024]{2,1,0:T(8,128)}) custom-call(bf16[32,512]{1,0:T(8,128)(2,1)S(1)} %get-tuple-element.9.student, bf16[3,192,256]{2,1,0:T(8,128)(2,1)S(1)} %get-tuple-element.10.grads, bf16[2,2,8,16,512]{4,3,2,1,0:T(8,128)(2,1)S(1)} %get-tuple-element.11.rows, ...), custom_call_target="tpu_custom_call" | custom-call | tf_op jit(solution)/shard_map/pallas_call | solution.py:473

commit v8 on v6

--- a/solution.py
+++ b/solution.py
@@ -115,7 +115,7 @@
     n_inner, n_outer,
     tokens_ref, teacher_ref, ids_ref, codes_ref, gu_ref, dn_ref,
     student, grads, rows, resid, latent, slope,
-    teacher, ids, codes, resid_own, gates_own, gates, weight, factor, sums, returned,
+    tokens, teacher, ids, codes, resid_own, gates_own, gates, weight, factor, sums, returned,
     load_sem, gate_send, gate_recv, tok_send, tok_recv, pair_send, pair_recv,
     sum_send, sum_recv, res_send, res_recv, res_rep,
 ):
@@ -148,9 +148,7 @@
         pltpu.make_async_copy(gu_ref.at[0, 0], latent.at[0], load_sem.at[0]),
         pltpu.make_async_copy(gu_ref.at[0, 1], latent.at[1], load_sem.at[1]),
         pltpu.make_async_copy(dn_ref.at[0], latent.at[2], load_sem.at[2]),
-        pltpu.make_async_copy(
-            tokens_ref.at[part_rows(rep)], rows.at[rep, rep, me], load_sem.at[3]
-        ),
+        pltpu.make_async_copy(tokens_ref, tokens, load_sem.at[3]),
         pltpu.make_async_copy(teacher_ref, teacher, load_sem.at[4]),
         pltpu.make_async_copy(ids_ref, ids, load_sem.at[5]),
         pltpu.make_async_copy(codes_ref, codes, load_sem.at[6]),
@@ -159,7 +157,7 @@
     for step, side in others:
         device = dict(peer_at(step)[1], rep=sides[side])
         pl.semaphore_signal(barrier, inc=1, device_id=device, device_id_type=MESH)
-    for load in loads:
+    for load in loads[3:] + loads[:3]:
         load.start()
     pl.semaphore_wait(barrier, len(others))
 
@@ -183,8 +181,9 @@
         ).wait_recv()
 
     mine = rep * n + me
+    loads[3].wait()
     spread(
-        lambda peer, side: tokens_ref.at[part_rows(side)],
+        lambda peer, side: tokens.at[part_rows(side)],
         lambda side: rows.at[side, rep, me],
         tok_send, tok_recv, mine,
     )
@@ -280,10 +279,10 @@
         factor[0, half] = gate_row * pre_up * sigmoid_gate * (1.0 + pre_gate * (1.0 - sigmoid_gate))
         factor[1, half] = gate_row * activated
 
-    loads[3].wait()
+    rows[rep, rep, me] = tokens[part_rows(rep), :]
     for step, side in others:
         arrived(
-            tokens_ref.at[part_rows(0)], lambda side, peer: rows.at[rep, side, peer],
+            tokens.at[part_rows(0)], lambda side, peer: rows.at[rep, side, peer],
             tok_send, tok_recv, step, side,
         )
     own_values = forward(rep, rep, own_gate)
@@ -331,21 +330,22 @@
     )
     resid[rep, rep, me] = resid_own[rep]
 
-    def pass_on(column, peer, at):
+    passed = []
+    for side in (1, 0):
+        for step, of in others:
+            if of == side:
+                arrived(
+                    resid_own.at[0], lambda side, peer: resid.at[rep, side, peer],
+                    res_send, res_recv, step, side,
+                )
+        column = sides[side]
         copy = remote(
-            resid.at[rep, column, peer], resid.at[rep, column, peer],
-            res_send.at[2 * n + at], res_rep.at[column * n + peer], partner,
+            resid.at[rep, column], resid.at[rep, column],
+            res_send.at[2 * n + side], res_rep.at[side], partner,
         )
         copy.start()
-        sent.append(copy)
-
-    pass_on(rep, me, 2 * n - 1)
-    for at, (step, side) in enumerate(others):
-        arrived(
-            resid_own.at[0], lambda side, peer: resid.at[rep, side, peer],
-            res_send, res_recv, step, side,
-        )
-        pass_on(sides[side], peer_at(-step)[0], at)
+        passed.append(copy)
+    sent.extend(passed)
 
     def backward(half):
         down = weight[rep, 2]
@@ -356,12 +356,8 @@
         grads[1, :, cols] = (hidden_grad * factor[1, half]).astype(BF16)
 
     backward(rep)
-    for column in range(2):
-        for peer in range(n):
-            remote(
-                resid_own.at[0], resid.at[1 - rep, column, peer],
-                res_send.at[0], res_rep.at[column * n + peer], partner,
-            ).wait_recv()
+    for copy in passed:
+        copy.wait_recv()
     backward(1 - rep)
     for copy in sent:
         copy.wait_send()
@@ -419,6 +415,7 @@
         out_specs=(vmem,) * 6,
         scratch_shapes=[
             pltpu.VMEM((tok_rows, width), BF16),
+            pltpu.VMEM((tok_rows, width), BF16),
             pltpu.VMEM(expert_ids.shape[::-1], jnp.int32),
             pltpu.VMEM(expert_ids.shape[::-1], jnp.int32),
             pltpu.VMEM((2, part, width), BF16),
@@ -437,9 +434,9 @@
             dma((4,)),
             dma((2 * n,)),
             dma((2 * n,)),
-            dma((4 * n,)),
+            dma((2 * n + 2,)),
             dma((2 * n,)),
-            dma((2 * n,)),
+            dma((2,)),
         ],
         compiler_params=pltpu.CompilerParams(
             collective_id=0, has_side_effects=True, vmem_limit_bytes=24 * 1024 * 1024

time: 34.4 us -> 34 us (0.988)
  Pallas kernels: 33.6 us -> 33.2 us
    pallas_call x1, Pallas kernels: 31.9 us -> 31.5 us  [dense_step(): pl.pallas_call(functools.partial(dense_kernel, n_inner, n_outer), out_sha...]
where the time goes in v8:
time: 34 us; the launch traced here: 33.9 us
  Pallas kernels  33.2 us (98%)
  between operations  0.64 us (2%)
    pallas_call x1, Pallas kernels, dense_step(): pl.pallas_call(functools.partial(dense_kernel, n_inner, n_outer), out_sha...  31.5 us
    pallas_call x1, Pallas kernels, dense_step(): pl.pallas_call(update_kernel, out_shape=(jax.ShapeDtypeStruct(tokens.shap...  1.72 us

profile of v8, /device:TPU:0, one launch (start us, length us, event | category | flops | bytes accessed | tf_op | source)
XLA Modules:
  0.0 33.9 jit_solution(17148639384833111643)
XLA Ops:
  0.6 31.5 %shard_map.85 = (bf16[32,512]{1,0:T(8,128)(2,1)S(1)}, bf16[3,192,256]{2,1,0:T(8,128)(2,1)S(1)}, bf16[2,2,8,16,512]{4,3,2,1,0:T(8,128)(2,1)S(1)}, bf16[2,2,8,16,5...) custom-call(bf16[32,512]{1,0:T(8,128)(2,1)} %tokens_ref.1, ...), custom_call_target="tpu_custom_call" | custom-call | tf_op jit(solution)/shard_map/pallas_call | solution.py:404
  32.2 1.7 %shard_map.86 = (bf16[32,512]{1,0:T(8,128)(2,1)}, f32[1,2,192,1024]{3,2,1,0:T(8,128)}, f32[1,192,1024]{2,1,0:T(8,128)}) custom-call(bf16[32,512]{1,0:T(8,128)(2,1)S(1)} %get-tuple-element.9.student, bf16[3,192,256]{2,1,0:T(8,128)(2,1)S(1)} %get-tuple-element.10.grads, bf16[2,2,8,16,512]{4,3,2,1,0:T(8,128)(2,1)S(1)} %get-tuple-element.11.rows, ...), custom_call_target="tpu_custom_call" | custom-call | tf_op jit(solution)/shard_map/pallas_call | solution.py:445

commit v9 on v8

--- a/solution.py
+++ b/solution.py
@@ -140,6 +140,7 @@
         )
 
     others = [(step, side) for step in range(n) for side in range(2) if step or side]
+    others.sort(key=lambda pair: abs(pair[0] - n // 2))
 
     def part_rows(side):
         return pl.ds(pl.multiple_of(side * part, part), part)

time: 34 us -> 36.3 us (1.068)
  Pallas kernels: 33.2 us -> 35.5 us
    pallas_call x1, Pallas kernels: 31.5 us -> 33.8 us  [dense_step(): pl.pallas_call(functools.partial(dense_kernel, n_inner, n_outer), out_sha...]
where the time goes in v9:
time: 36.3 us; the launch traced here: 36.2 us
  Pallas kernels  35.5 us (98%)
  between operations  0.64 us (2%)
    pallas_call x1, Pallas kernels, dense_step(): pl.pallas_call(functools.partial(dense_kernel, n_inner, n_outer), out_sha...  33.8 us
    pallas_call x1, Pallas kernels, dense_step(): pl.pallas_call(update_kernel, out_shape=(jax.ShapeDtypeStruct(tokens.shap...  1.72 us

profile of v9, /device:TPU:0, one launch (start us, length us, event | category | flops | bytes accessed | tf_op | source)
XLA Modules:
  0.0 36.2 jit_solution(8237284493746963702)
XLA Ops:
  0.6 33.8 %shard_map.85 = (bf16[32,512]{1,0:T(8,128)(2,1)S(1)}, bf16[3,192,256]{2,1,0:T(8,128)(2,1)S(1)}, bf16[2,2,8,16,512]{4,3,2,1,0:T(8,128)(2,1)S(1)}, bf16[2,2,8,16,5...) custom-call(bf16[32,512]{1,0:T(8,128)(2,1)} %tokens_ref.1, ...), custom_call_target="tpu_custom_call" | custom-call | tf_op jit(solution)/shard_map/pallas_call | solution.py:405
  34.5 1.7 %shard_map.86 = (bf16[32,512]{1,0:T(8,128)(2,1)}, f32[1,2,192,1024]{3,2,1,0:T(8,128)}, f32[1,192,1024]{2,1,0:T(8,128)}) custom-call(bf16[32,512]{1,0:T(8,128)(2,1)S(1)} %get-tuple-element.9.student, bf16[3,192,256]{2,1,0:T(8,128)(2,1)S(1)} %get-tuple-element.10.grads, bf16[2,2,8,16,512]{4,3,2,1,0:T(8,128)(2,1)S(1)} %get-tuple-element.11.rows, ...), custom_call_target="tpu_custom_call" | custom-call | tf_op jit(solution)/shard_map/pallas_call | solution.py:446
